TPU v7x, 32 devices: a whole 2x2x4 slice. The times are simulated.
32 devices in a mesh: stream: 4 (over y, x), seq: 8 (over z, core).
Axes of the slice: x: 2, y: 2, z: 4, core: 2. Of those that a mesh axis runs over, the one named last changes fastest.
Arguments:
- conv_input: bfloat16 [4, 32768, 1280], P('stream', 'seq'), may hold values from -6 to 6
- conv_weight: float32 [4, 1280], replicated, may hold values from -3 to 3
- conv_bias: float32 [1280], replicated, may hold values from -1 to 1
- step_size: float32 [4, 16, 32768], P('stream', None, 'seq'), may hold values from 0.0005 to 0.005
- log_decay: float32 [4, 16, 32768], P('stream', None, 'seq'), as said below
- skip_gain: float32 [16], replicated, may hold values from 0.5 to 1.5
- doc_bounds: int32 [4, 32], P('stream'), may hold values from 1 to 32768, as said below
- doc_owner: int32 [4, 32], P('stream'), may hold values from 0 to 3, as said below
Outputs:
- mixed_out: bfloat16 [4, 32768, 1024], P('stream', 'seq')
- handoff_ssm: float32 [4, 8, 4, 2, 16, 64, 128], P('stream', 'seq')
- handoff_conv: bfloat16 [4, 8, 4, 2, 3, 1280], P('stream', 'seq')
Inputs may be any that keep to these rules, and one draw needn't show every extreme that they name: `doc_bounds`: each row rises and never falls; the real documents of a stream end at 32768, after which every entry equals 32768. At most 4 real documents have their last position in one run of 4096 positions starting at a multiple of 4096. `doc_owner`: among the real documents whose last positions lie in one such run of one stream, no owner is named more than 2 times. `log_decay`: never positive.
All inputs are finite; a program needn't handle non-finite values.
Results may differ from a plain program's by a relative error of at most 0.006.
Values may be sent and summed in bfloat16 or wider, within the bound.
No kernel may reach another device: no remote copies, remote signals or barrier semaphores. Data moves between devices by JAX's collectives and lax.ppermute only.
A program may use at most 256 MiB of HBM per device.

v0:
```python
import functools

import jax
import jax.numpy as jnp
import numpy as np
from jax import lax
from jax.experimental import pallas as pl
from jax.experimental.pallas import tpu as pltpu
from jax.sharding import PartitionSpec as P

P_SIZE = 64
N = 128
EMAX = 4
CAP = 2
CHUNK = 128
BLOCK = 512
FAR = 1 << 30
LOG2E = 1.4426950408889634
PAY = 144
TAIL = 32
MIB = 1024 * 1024

F32 = jnp.float32
BF16 = jnp.bfloat16


def shifted(value, axis, steps):
    count = lax.axis_size(axis)
    leading, last = (max(0, -steps), min(count, count - steps))
    return lax.ppermute(value, axis, [(source, source + steps) for source in range(leading, last)])


def iota(shape, axis):
    return lax.broadcasted_iota(jnp.int32, shape, axis)


def outer_dot(left, right):
    return lax.dot_general(left, right, (((0,), (0,)), ((), ())), preferred_element_type=F32)


def halves(value):
    high = value.astype(BF16)
    low = (value - high.astype(F32)).astype(BF16)
    return jnp.concatenate([high, low], axis=0)


def thirds(value):
    high = value.astype(BF16)
    rest = value - high.astype(F32)
    mid = rest.astype(BF16)
    low = (rest - mid.astype(F32)).astype(BF16)
    return jnp.concatenate([high, mid, low], axis=0)


def spread_row(column, rep):
    return jnp.sum(rep * column, axis=0, keepdims=True)


def last_start(meta, place):
    start = meta[0]
    for slot in range(EMAX):
        end = meta[1 + slot]
        start = jnp.where(end <= place, end, start)
    return start


def next_end(meta, place):
    end = FAR
    for slot in reversed(range(EMAX)):
        end = jnp.where(meta[1 + slot] > place, meta[1 + slot], end)
    return end


def starts_of(meta, rows):
    start = jnp.full(rows.shape, meta[0], jnp.int32)
    for slot in range(EMAX):
        end = meta[1 + slot]
        start = jnp.where(rows >= end, end, start)
    return start


def read_docs(bounds, owners, meta, count, anchor, span):
    for slot in range(EMAX):
        meta[1 + slot] = FAR
        meta[5 + slot] = 0
    for owner in range(count.shape[0]):
        count[owner] = 0

    def one(index, carry):
        found, prior, start = carry
        end = bounds[0, index]
        owner = owners[0, index]
        mine = (end > prior) & (end > anchor) & (end <= anchor + span) & (found < EMAX)

        @pl.when(mine)
        def _():
            meta[1 + found] = end - anchor
            rank = count[owner]
            meta[5 + found] = jnp.where(rank < CAP, owner * CAP + rank, -1)
            count[owner] = rank + 1

        return found + mine.astype(jnp.int32), end, jnp.where(end <= anchor, end, start)

    zero = jnp.int32(0)
    _, _, start = lax.fori_loop(0, bounds.shape[1], one, (zero, zero, zero))
    meta[0] = start - anchor


def conv_kernel(
    shard_ref, bounds, owners, x_ref, rim_ref, w_ref, bias_ref, move_ref, slot_ref,
    act_ref, b_ref, c_ref, meta,
    edge16, weights, moves, count,
):
    step = pl.program_id(0)
    span = pl.num_programs(0) * BLOCK
    parts = BLOCK // CHUNK
    first = step * BLOCK

    @pl.when(step == 0)
    def _():
        read_docs(bounds, owners, meta, count, shard_ref[0] * span, span)
        edge16[...] = rim_ref[...]
        weights[0:4] = 0.5 * w_ref[...]
        weights[4:5] = 0.5 * bias_ref[...].reshape(1, weights.shape[1])
        moves[0] = move_ref[...]

    choices = []
    for part in range(parts):
        begin = first + part * CHUNK
        near = (meta[0] > begin - 3) & (meta[0] < begin + CHUNK)
        for slot in range(EMAX):
            near = near | ((meta[1 + slot] > begin - 3) & (meta[1 + slot] < begin + CHUNK))

        @pl.when(near)
        def _():
            tick = slot_ref[...] // 4 + begin
            kept = (tick - starts_of(meta, tick) >= slot_ref[...] % 4).astype(F32)
            moves[1 + part, :, :128] = (kept * move_ref[:, :128].astype(F32)).astype(BF16)
            moves[1 + part, :, 128:] = (kept[:, :16] * move_ref[:, 128:].astype(F32)).astype(BF16)

        choices.append(jnp.where(near, 1 + part, 0))

    for part in range(parts):
        low = part * CHUNK
        rows = slice(low, low + CHUNK)
        pick = moves[choices[part]]
        for tile in range(x_ref.shape[1] // 256):
            cols = slice(tile * 256, tile * 256 + 256)
            if part:
                wide = x_ref[low - 16 : low + CHUNK, cols]
            else:
                wide = jnp.concatenate([edge16[:, cols], x_ref[rows, cols]], axis=0)
            moved = jnp.dot(pick, wide, preferred_element_type=F32)
            moved = moved.reshape(CHUNK // 8, 3, 8, 256)
            mixed = weights[4:5, cols] + weights[0:1, cols] * x_ref[rows, cols].astype(F32)
            for lag in range(1, 4):
                mixed = mixed + weights[lag : lag + 1, cols] * moved[:, lag - 1].reshape(CHUNK, 256)
            value = (mixed + mixed * jnp.tanh(mixed)).astype(BF16)
            if tile * 256 < act_ref.shape[1]:
                act_ref[rows, cols] = value
            else:
                b_ref[rows, :] = value[:, :N]
                c_ref[rows, :] = value[:, N:]

    edge16[...] = x_ref[BLOCK - 16 :, :]


def states_kernel(
    meta, act_ref, b_ref, dt_ref, ld_ref, rep_ref, rep16_ref, tri_ref,
    cum_ref, carry_ref, sin_ref, pay_ref,
    state, total,
):
    step = pl.program_id(0)
    heads = dt_ref.shape[0]
    width = rep_ref.shape[1]
    span = pl.num_programs(0) * BLOCK
    parts = BLOCK // CHUNK
    first = step * BLOCK

    @pl.when(step == 0)
    def _():
        state[...] = jnp.zeros_like(state)
        total[...] = jnp.zeros_like(total)

    spans = [slice(part * CHUNK, part * CHUNK + CHUNK) for part in range(parts)]
    pieces = jnp.concatenate([thirds(ld_ref[:, rows] * LOG2E) for rows in spans], axis=0)
    summed = jnp.dot(pieces, tri_ref[...], preferred_element_type=F32)
    open_end = jnp.where(meta[0] < 0, meta[1], -1)
    running = total[...]
    weights = []
    throughs = []
    for part, rows in enumerate(spans):
        begin = first + part * CHUNK
        at = 3 * heads * part
        cum = summed[at : at + heads] + summed[at + heads : at + 2 * heads] + summed[at + 2 * heads : at + 3 * heads]
        cum_ref[:, rows] = cum
        lane = iota((heads, CHUNK), 1) + begin
        carry_ref[:, rows] = jnp.where(lane < open_end, jnp.exp2(running + cum), 0.0)
        start = last_start(meta, begin + CHUNK - 1)
        last = cum[:, CHUNK - 1 :]
        weight = jnp.where(lane >= start, jnp.exp2(last - cum) * dt_ref[:, rows], 0.0)
        weights.append(weight.T.astype(BF16))
        throughs.append(spread_row(jnp.where(start < begin, jnp.exp2(last), 0.0), rep_ref[...]))
        running = running + last
    total[...] = running
    weight = jnp.concatenate(weights, axis=0)
    turned = [b_ref[rows, :].T for rows in spans]
    for tile in range(width // 256):
        cols = slice(tile * 256, tile * 256 + 256)
        scale = jnp.dot(weight, rep16_ref[:heads, cols], preferred_element_type=F32)
        load = scale.astype(BF16) * act_ref[:, cols]
        held = state[:, cols]
        for part, rows in enumerate(spans):
            sin_ref[part, :, cols] = held.astype(BF16)
            grown = jnp.dot(turned[part], load[rows], preferred_element_type=F32)
            held = throughs[part][:, cols] * held + grown
        state[:, cols] = held

    @pl.when(step == pl.num_programs(0) - 1)
    def _():
        start = last_start(meta, span - 1)
        gate = spread_row(jnp.where(start < 0, jnp.exp2(total[:, :1]), 0.0), rep_ref[...])
        gate = jnp.broadcast_to(gate, (PAY - N, width))
        high = gate.astype(BF16).astype(F32)
        pay_ref[:N] = state[...].astype(BF16)
        pay_ref[N:] = jnp.where(iota((PAY - N, width), 0) == 0, high, gate - high).astype(BF16)


def finals_kernel(
    meta, act_hbm, b_hbm, sin_hbm, x_hbm, rim_ref, dt_ref, cum_ref, carry_ref, rep_ref, rep16_ref,
    fin_hbm, first_ref,
    act_held, b_held, sin_held, x_held, edge_held, blank, made, lines, in_sem, blank_sem, made_sem,
):
    heads, span = dt_ref.shape
    width = rep_ref.shape[1]

    def place(slot):
        return pl.multiple_of((meta[1 + slot] - 1) // CHUNK * CHUNK, CHUNK)

    def copies(slot):
        low = place(slot)
        rows = pl.ds(low, CHUNK)
        before = pl.ds(pl.multiple_of(jnp.maximum(low - 16, 0), 16), 16)
        pairs = (
            (act_hbm.at[rows], act_held), (b_hbm.at[rows], b_held), (sin_hbm.at[low // CHUNK], sin_held),
            (x_hbm.at[rows], x_held), (x_hbm.at[before], edge_held),
        )
        return [
            pltpu.make_async_copy(source, target.at[slot], in_sem.at[slot, index])
            for index, (source, target) in enumerate(pairs)
        ]

    def fetch(slot, _):
        for copy in copies(slot):
            copy.start()
        return 0

    found = jnp.int32(0)
    for slot in range(EMAX):
        found = found + (meta[1 + slot] <= span).astype(jnp.int32)
    lax.fori_loop(0, found, fetch, 0)
    blank[...] = jnp.zeros_like(blank)
    blanks = [
        pltpu.make_async_copy(blank, fin_hbm.at[index], blank_sem.at[index])
        for index in range(fin_hbm.shape[0])
    ]
    for copy in blanks:
        copy.start()
    first_ref[...] = jnp.zeros_like(first_ref)
    lines[...] = jnp.zeros_like(lines)
    for copy in blanks:
        copy.wait()

    def finish(slot, _):
        for copy in copies(slot):
            copy.wait()
        end = meta[1 + slot]
        start = jnp.where(slot > 0, meta[jnp.maximum(slot, 1)], meta[0])
        low = place(slot)
        there = pl.ds(low, CHUNK)
        lane = iota((heads, CHUNK), 1) + low
        cum = cum_ref[:, there]
        at_end = jnp.sum(jnp.where(lane == end - 1, cum, 0.0), axis=1, keepdims=True)
        inside = (lane < end) & (lane >= start)
        weight = jnp.exp2(jnp.minimum(at_end - cum, 0.0)) * dt_ref[:, there]
        weight = jnp.where(inside, weight, 0.0).T.astype(BF16)
        scale = jnp.dot(weight, rep16_ref[:heads], preferred_element_type=F32)
        load = scale.astype(BF16) * act_held[slot]
        local = outer_dot(b_held[slot], load)
        through = spread_row(jnp.where(start < low, jnp.exp2(at_end), 0.0), rep_ref[...])
        final = local + through * sin_held[slot].astype(F32)
        target = meta[5 + slot]

        @pl.when((slot == 0) & (start < 0))
        def _():
            opened = jnp.sum(jnp.where(lane == end - 1, carry_ref[:, there], 0.0), axis=1, keepdims=True)
            first_ref[...] = jnp.broadcast_to(spread_row(opened, rep_ref[...]), first_ref.shape)

        row = iota((16, CHUNK), 0)
        col = iota((16, CHUNK), 1) + low
        pick = (col == end - 3 + row) & (col >= start) & (row < 3)
        row16 = iota((16, 16), 0)
        col16 = iota((16, 16), 1) + low - 16
        pick16 = (col16 == end - 3 + row16) & (col16 >= start) & (row16 < 3)
        rim = jnp.where(low > 0, edge_held[slot].astype(F32), rim_ref[...].astype(F32))
        last = jnp.dot(
            pick.astype(F32).astype(BF16), x_held[slot], preferred_element_type=F32
        ) + jnp.dot(pick16.astype(F32).astype(BF16), rim.astype(BF16), preferred_element_type=F32)
        tiles = x_held.shape[2] // 128
        for index in range(3):
            for tile in range(tiles):
                at = index * tiles + tile
                lines[at : at + 1] = last[index : index + 1, tile * 128 : tile * 128 + 128]

        @pl.when(target >= 0)
        def _():
            made[slot, :width] = final.astype(BF16).T
            made[slot, width:] = lines[...].astype(BF16)
            pltpu.make_async_copy(made.at[slot], fin_hbm.at[target], made_sem.at[slot]).start()

        return 0

    lax.fori_loop(0, found, finish, 0)

    def close(slot, _):
        @pl.when(meta[5 + slot] >= 0)
        def _():
            pltpu.make_async_copy(made.at[slot], fin_hbm.at[meta[5 + slot]], made_sem.at[slot]).wait()

        return 0

    lax.fori_loop(0, found, close, 0)


def output_kernel(origin, late, meta, act_ref, b_ref, c_ref, dt_ref, cum_ref, sin_ref, gain_in, rep_ref, rep16_ref, each_ref, *refs):
    out_ref, gain_ref = refs[-2:]
    step = origin + pl.program_id(0)
    heads = dt_ref.shape[0]
    width = out_ref.shape[1]
    parts = BLOCK // CHUNK

    @pl.when(pl.program_id(0) == 0)
    def _():
        row = jnp.zeros((1, width), F32)
        for head in range(heads):
            row = row + gain_in[head] * rep_ref[head : head + 1, :]
        gain_ref[...] = row

    for part in range(parts):
        begin = step * BLOCK + part * CHUNK
        rows = slice(part * CHUNK, part * CHUNK + CHUNK)
        cum = cum_ref[:, rows]
        back = cum - jnp.log2(dt_ref[:, rows])
        ahead = jnp.concatenate(
            [thirds(cum), jnp.ones((3 * heads, CHUNK), BF16), jnp.zeros((CHUNK - 6 * heads, CHUNK), BF16)], axis=0
        ).T
        back = thirds(-back)
        b_act = b_ref[rows, :]
        c_act = c_ref[rows, :]
        place = iota((CHUNK, CHUNK), 0) + begin
        other = iota((CHUNK, CHUNK), 1) + begin
        scores = lax.dot_general(c_act, b_act, (((1,), (1,)), ((), ())), preferred_element_type=F32)
        scores = jnp.where((other <= place) & (other >= starts_of(meta, place)), scores, 0.0)
        scores = jnp.concatenate([scores, scores], axis=1)
        blank = jnp.zeros((CHUNK - 6 * heads, 256), BF16)
        lane = iota((heads, CHUNK), 1) + begin
        before = jnp.where(last_start(meta, begin) < begin, next_end(meta, begin), -1)
        entry = jnp.where(lane < before, jnp.exp2(cum), 0.0)
        entry = jnp.concatenate([entry, entry - entry.astype(BF16).astype(F32)], axis=0).T.astype(BF16)
        if late:
            extra = refs[0][:, rows]
            extra = jnp.concatenate([extra, extra - extra.astype(BF16).astype(F32)], axis=0).T.astype(BF16)
        left_half = iota((CHUNK, 128), 1) < P_SIZE
        for quad in range(heads // 4):
            cols = slice(quad * 256, quad * 256 + 256)
            outer = jnp.dot(c_act, sin_ref[part, :, cols], preferred_element_type=F32)
            scale = jnp.dot(entry, rep16_ref[:, cols], preferred_element_type=F32)
            sums = []
            for pair in (2 * quad, 2 * quad + 1):
                own = each_ref[:, pair * 256 : pair * 256 + 256]
                against = jnp.concatenate([own, jnp.concatenate([back, back], axis=1) * own, blank], axis=0)
                spread = jnp.dot(ahead, against, preferred_element_type=F32)
                mix = (jnp.exp2(jnp.minimum(spread, 0.0)) * scores).astype(BF16)
                x_pair = act_ref[rows, pair * 128 : pair * 128 + 128]
                zero = jnp.zeros_like(x_pair)
                split = jnp.concatenate(
                    [jnp.where(left_half, x_pair, zero), jnp.where(left_half, zero, x_pair)], axis=0
                )
                sums.append(jnp.dot(mix, split, preferred_element_type=F32))
            inner = jnp.concatenate(sums, axis=1)
            value = inner + scale * outer + gain_ref[:, cols] * act_ref[rows, cols].astype(F32)
            if late:
                outer = jnp.dot(c_act, refs[1][:, cols], preferred_element_type=F32)
                scale = jnp.dot(extra, rep16_ref[:, cols], preferred_element_type=F32)
                value = value + scale * outer
            out_ref[rows, cols] = value.astype(BF16)


def gates_of(pay_ref, cols):
    gates = pay_ref[N:, cols].astype(F32)
    return gates[0:1] + gates[1:2]


def pair_kernel(shard_ref, own_ref, got_ref, half_ref):
    side = half_ref.shape[1]

    def join(early, late, cols):
        after = gates_of(late, cols)
        gate = jnp.broadcast_to(after * gates_of(early, cols), (PAY - N, side))
        high = gate.astype(BF16).astype(F32)
        half_ref[:N] = (late[:N, cols].astype(F32) + after * early[:N, cols].astype(F32)).astype(BF16)
        half_ref[N:] = jnp.where(iota((PAY - N, side), 0) == 0, high, gate - high).astype(BF16)

    @pl.when(shard_ref[0] % 2 == 0)
    def _():
        join(own_ref, got_ref, slice(0, side))

    @pl.when(shard_ref[0] % 2 == 1)
    def _():
        join(got_ref, own_ref, slice(side, 2 * side))


def prefix_kernel(*refs):
    prefix_ref = refs[-1]
    side = prefix_ref.shape[1]
    total = jnp.zeros((N, side), F32)
    for ref in refs[:-1]:
        total = gates_of(ref, slice(0, side)) * total + ref[:N].astype(F32)
    prefix_ref[...] = total.astype(BF16)


def carry_kernel(shard_ref, stream_ref, meta, mine_ref, other_ref, early_ref, first_ref, carried_ref, *sends):
    side = mine_ref.shape[1]
    lower, upper = slice(0, side), slice(side, 2 * side)

    @pl.when(shard_ref[0] % 2 == 0)
    def _():
        carried_ref[:, lower] = mine_ref[...]
        carried_ref[:, upper] = other_ref[...]

    @pl.when(shard_ref[0] % 2 == 1)
    def _():
        for cols, part in ((lower, other_ref), (upper, mine_ref)):
            carried_ref[:, cols] = (
                early_ref[:N, cols].astype(F32) + gates_of(early_ref, cols) * part[...].astype(F32)
            ).astype(BF16)

    value = (first_ref[0:1] * carried_ref[...].astype(F32)).T.astype(BF16)
    apart = (meta[5] // CAP) ^ stream_ref[0]
    for index, ref in enumerate(sends):
        ref[...] = jnp.where(apart == index, value, jnp.zeros_like(value))


def correct_kernel(meta, base_hbm, c_ref, carry_ref, carried_ref, rep16_ref, out_hbm, held, in_sem, out_sem):
    steps, _, width = held.shape
    reach = jnp.where(meta[0] < 0, jnp.minimum(meta[1], steps * BLOCK), 0)
    touched = (reach + BLOCK - 1) // BLOCK

    def copy(index, source, target, sem):
        place = pl.ds(pl.multiple_of(index * BLOCK, BLOCK), BLOCK)
        if source is held:
            return pltpu.make_async_copy(held.at[index], target.at[place], sem.at[index])
        return pltpu.make_async_copy(source.at[place], held.at[index], sem.at[index])

    def fetch(index, _):
        copy(index, base_hbm, held, in_sem).start()
        return 0

    def add(index, _):
        copy(index, base_hbm, held, in_sem).wait()
        rows = pl.ds(pl.multiple_of(index * BLOCK, BLOCK), BLOCK)
        entry = carry_ref[:, rows]
        entry = jnp.concatenate([entry, entry - entry.astype(BF16).astype(F32)], axis=0).T.astype(BF16)
        c_act = c_ref[rows, :]
        for tile in range(width // 256):
            cols = slice(tile * 256, tile * 256 + 256)
            outer = jnp.dot(c_act, carried_ref[:, cols], preferred_element_type=F32)
            scale = jnp.dot(entry, rep16_ref[:, cols], preferred_element_type=F32)
            held[index, :, cols] = (held[index, :, cols].astype(F32) + scale * outer).astype(BF16)
        copy(index, held, out_hbm, out_sem).start()
        return 0

    def close(index, _):
        copy(index, held, out_hbm, out_sem).wait()
        return 0

    lax.fori_loop(0, touched, fetch, 0)
    lax.fori_loop(0, touched, add, 0)
    lax.fori_loop(0, touched, close, 0)


def params(mib):
    return pltpu.CompilerParams(vmem_limit_bytes=mib * MIB)


def whole(shape):
    return pl.BlockSpec(shape, lambda *_: (0,) * len(shape))


def on_device(
    conv_input, conv_weight, conv_bias, step_size, log_decay, skip_gain, doc_bounds, doc_owner
):
    span, channels = conv_input.shape[1:]
    heads = step_size.shape[1]
    width = heads * P_SIZE
    steps = span // BLOCK
    chunks = span // CHUNK
    owners = lax.axis_size("stream")
    slots = owners * CAP
    rows = width + TAIL
    shard = lax.axis_index("seq").astype(jnp.int32).reshape(1)
    rows_in = conv_input[0]
    rim = shifted(rows_in[span - 16 :], "seq", 1)
    rep = (np.arange(width)[None, :] // P_SIZE == np.arange(heads)[:, None]).astype(np.float32)
    rep16 = np.concatenate([rep, rep], 0).astype(BF16)
    each = np.arange(heads * CHUNK)[None, :] // CHUNK == np.arange(3 * heads)[:, None] % heads
    each = each.astype(BF16)
    ticks = np.arange(CHUNK)
    tri = (ticks[:, None] <= ticks[None, :]).astype(BF16)
    order = np.arange(3 * CHUNK)
    tick, lag = 8 * (order // 24) + order % 8, order % 24 // 8 + 1
    source = np.arange(CHUNK + 16)
    move = (source[None, :] - 16 == (tick - lag)[:, None]).astype(BF16)
    slot = np.broadcast_to((4 * tick + lag)[:, None], (3 * CHUNK, 128)).astype(np.int32)
    smem = pl.BlockSpec(memory_space=pltpu.SMEM)
    stream = lax.axis_index("stream").astype(jnp.int32).reshape(1)
    per_head = pl.BlockSpec((heads, BLOCK), lambda i, *_: (0, i))
    prefetch = functools.partial(pltpu.PrefetchScalarGridSpec, num_scalar_prefetch=1)
    by_rows = pl.BlockSpec((BLOCK, channels), lambda i, *_: (i, 0))
    by_width = pl.BlockSpec((BLOCK, width), lambda i, *_: (i, 0))
    by_rest = pl.BlockSpec((BLOCK, N), lambda i, *_: (i, 0))
    act, b_act, c_act, meta = pl.pallas_call(
        conv_kernel,
        grid=(steps,),
        in_specs=[
            smem, smem, smem, by_rows, whole((16, channels)),
            whole((4, channels)), whole((channels,)), whole(move.shape), whole(slot.shape),
        ],
        out_specs=[by_width, by_rest, by_rest, smem],
        out_shape=[
            jax.ShapeDtypeStruct((span, width), BF16),
            jax.ShapeDtypeStruct((span, N), BF16),
            jax.ShapeDtypeStruct((span, N), BF16),
            jax.ShapeDtypeStruct((16,), jnp.int32),
        ],
        scratch_shapes=[
            pltpu.VMEM((16, channels), BF16),
            pltpu.VMEM((8, channels), F32),
            pltpu.VMEM((1 + BLOCK // CHUNK,) + move.shape, BF16),
            pltpu.SMEM((owners,), jnp.int32),
        ],
        compiler_params=params(60),
        cost_estimate=pl.CostEstimate(
            flops=2 * span * channels * 400, bytes_accessed=21 << 20, transcendentals=span * channels
        ),
        name="conv",
    )(shard, doc_bounds, doc_owner, rows_in, rim, conv_weight, conv_bias, move, slot)
    in_hbm = pl.BlockSpec(memory_space=pl.ANY)
    cum, carry, sin, pay = pl.pallas_call(
        states_kernel,
        grid_spec=prefetch(
            grid=(steps,),
            in_specs=[
                by_width, by_rest, per_head, per_head,
                whole((heads, width)), whole((2 * heads, width)), whole((CHUNK, CHUNK)),
            ],
            out_specs=[
                per_head, per_head,
                pl.BlockSpec((BLOCK // CHUNK, N, width), lambda i, *_: (i, 0, 0)),
                whole((PAY, width)),
            ],
            scratch_shapes=[
                pltpu.VMEM((N, width), F32),
                pltpu.VMEM((heads, CHUNK), F32),
            ],
        ),
        out_shape=[
            jax.ShapeDtypeStruct((heads, span), F32),
            jax.ShapeDtypeStruct((heads, span), F32),
            jax.ShapeDtypeStruct((chunks, N, width), BF16),
            jax.ShapeDtypeStruct((PAY, width), BF16),
        ],
        compiler_params=params(60),
        cost_estimate=pl.CostEstimate(
            flops=2 * span * width * N * 2, bytes_accessed=22 << 20, transcendentals=span * heads
        ),
        name="states",
    )(meta, act, b_act, step_size[0], log_decay[0], rep, rep16, tri)


    def outputs(first, last, late=()):
        rows_of = functools.partial(pl.BlockSpec, index_map=lambda i, *_: (first + i, 0))
        heads_of = pl.BlockSpec((heads, BLOCK), lambda i, *_: (0, first + i))
        return pl.pallas_call(
            functools.partial(output_kernel, first, bool(late)),
            grid_spec=prefetch(
                grid=(last - first,),
                in_specs=[
                    rows_of((BLOCK, width)), rows_of((BLOCK, N)), rows_of((BLOCK, N)), heads_of, heads_of,
                    pl.BlockSpec((BLOCK // CHUNK, N, width), lambda i, *_: (first + i, 0, 0)),
                    smem, whole((heads, width)), whole((2 * heads, width)), whole(each.shape),
                ] + ([heads_of, whole((N, width)), pl.BlockSpec(memory_space=pl.ANY)] if late else []),
                out_specs=rows_of((BLOCK, width)),
                scratch_shapes=[pltpu.VMEM((1, width), F32)],
            ),
            out_shape=jax.ShapeDtypeStruct((span, width), BF16),
            input_output_aliases={13: 0} if late else {},
            compiler_params=params(60),
            cost_estimate=pl.CostEstimate(
                flops=2 * (last - first) * BLOCK * width * N * 4,
                bytes_accessed=(last - first) * (4 << 20),
                transcendentals=(last - first) * BLOCK * CHUNK * heads,
            ),
            name="outputs",
        )(meta, act, b_act, c_act, step_size[0], cum, sin, skip_gain, rep, rep16, each, *late)

    side = width // 2
    count = lax.axis_size("seq")
    pairs = [(index, index ^ 1) for index in range(count)]
    early = lax.ppermute(pay, "seq", pairs)
    half = pl.pallas_call(
        pair_kernel,
        in_specs=[smem, whole((PAY, width)), whole((PAY, width))],
        out_specs=whole((PAY, side)),
        out_shape=jax.ShapeDtypeStruct((PAY, side), BF16),
        compiler_params=params(8),
        name="pair",
    )(shard, pay, early)
    chips = count // 2
    behind = [shifted(half, "seq", 2 * far) for far in range(chips - 1, 0, -1)]
    scanned, half = lax.optimization_barrier((sin, half))
    fin, first = pl.pallas_call(
        finals_kernel,
        in_specs=[
            smem, in_hbm, in_hbm, in_hbm, in_hbm, whole((16, channels)),
            whole((heads, span)), whole((heads, span)), whole((heads, span)),
            whole((heads, width)), whole((2 * heads, width)),
        ],
        out_specs=[in_hbm, whole((8, width))],
        out_shape=[
            jax.ShapeDtypeStruct((slots, rows, N), BF16),
            jax.ShapeDtypeStruct((8, width), F32),
        ],
        scratch_shapes=[
            pltpu.VMEM((EMAX, CHUNK, width), BF16),
            pltpu.VMEM((EMAX, CHUNK, N), BF16),
            pltpu.VMEM((EMAX, N, width), BF16),
            pltpu.VMEM((EMAX, CHUNK, channels), BF16),
            pltpu.VMEM((EMAX, 16, channels), BF16),
            pltpu.VMEM((rows, N), BF16),
            pltpu.VMEM((EMAX, rows, N), BF16),
            pltpu.VMEM((TAIL, N), F32),
            pltpu.SemaphoreType.DMA((EMAX, 5)),
            pltpu.SemaphoreType.DMA((slots,)),
            pltpu.SemaphoreType.DMA((EMAX,)),
        ],
        compiler_params=params(58),
        cost_estimate=pl.CostEstimate(flops=1 << 28, bytes_accessed=6 << 20, transcendentals=0),
        name="finals",
    )(meta, act, b_act, scanned, rows_in, rim, step_size[0], cum, carry, rep, rep16)
    sin, fin = lax.optimization_barrier((sin, fin))
    got = lax.all_to_all(
        fin.reshape(owners, CAP, rows, N), "stream", split_axis=0, concat_axis=0, tiled=True
    )
    base = outputs(0, steps)
    *behind, base = lax.optimization_barrier((*behind, base))
    mine = pl.pallas_call(
        prefix_kernel,
        in_specs=[whole((PAY, side))] * len(behind),
        out_specs=whole((N, side)),
        out_shape=jax.ShapeDtypeStruct((N, side), BF16),
        compiler_params=params(8),
        name="prefix",
    )(*behind)
    other = lax.ppermute(mine, "seq", pairs)
    other, got = lax.optimization_barrier((other, got))
    carried, *send = pl.pallas_call(
        carry_kernel,
        in_specs=[smem, smem, smem, whole((N, side)), whole((N, side)), whole((PAY, width)), whole((8, width))],
        out_specs=[whole((N, width))] + [whole((width, N))] * owners,
        out_shape=[jax.ShapeDtypeStruct((N, width), BF16)]
        + [jax.ShapeDtypeStruct((width, N), BF16)] * owners,
        compiler_params=params(8),
        name="carry",
    )(shard, stream, meta, mine, other, early, first)
    more = [send[0]]
    for apart in range(1, owners):
        swap = [(index, index ^ apart) for index in range(owners)]
        more.append(lax.ppermute(send[apart], "stream", swap))

    out = pl.pallas_call(
        correct_kernel,
        in_specs=[smem, in_hbm, whole((span, N)), whole((heads, span)), whole((N, width)), whole((2 * heads, width))],
        out_specs=in_hbm,
        out_shape=jax.ShapeDtypeStruct((span, width), BF16),
        scratch_shapes=[
            pltpu.VMEM((steps, BLOCK, width), BF16),
            pltpu.SemaphoreType.DMA((steps,)),
            pltpu.SemaphoreType.DMA((steps,)),
        ],
        input_output_aliases={1: 0},
        compiler_params=params(58),
        cost_estimate=pl.CostEstimate(
            flops=2 * span * width * N, bytes_accessed=18 << 20, transcendentals=0
        ),
        name="correct",
    )(meta, base, c_act, carry, carried, rep16)

    apart = (jnp.arange(owners) ^ stream)[:, None, None]
    extra = jnp.broadcast_to(more[0][None], (owners, width, N))
    for index in range(1, owners):
        extra = jnp.where(apart == index, more[index][None], extra)
    ranks = jnp.arange(CAP)[None, :, None, None]
    extra = jnp.where(ranks == 0, extra[:, None], jnp.zeros_like(extra[:, None]))
    ssm = got[:, :, :width].astype(F32) + extra.astype(F32)
    ssm = ssm.reshape(1, 1, owners, CAP, heads, P_SIZE, N)
    tiles = channels // N
    conv = got[:, :, width : width + 3 * tiles].reshape(1, 1, owners, CAP, 3, channels)
    return out[None], ssm, conv


def solution(mesh):
    in_specs = (
        P("stream", "seq", None),
        P(),
        P(),
        P("stream", None, "seq"),
        P("stream", None, "seq"),
        P(),
        P("stream", None),
        P("stream", None),
    )
    out_specs = (
        P("stream", "seq", None),
        P("stream", "seq", None, None, None, None, None),
        P("stream", "seq", None, None, None, None),
    )
    return jax.shard_map(
        on_device, mesh=mesh, in_specs=in_specs, out_specs=out_specs, check_vma=False
    )
```

profile of v0, /device:TPU:0, one launch (start us, length us, event | category | flops | bytes accessed | tf_op | source)
XLA Modules:
  0.0 106.4 jit_solution(12586309715006160639)
XLA Ops:
  0.6 0.8 slice_bitcast_fusion
  1.4 2.3 %collective-permute-start = (bf16[16,1280]{1,0:T(8,128)(2,1)S(1)}, bf16[16,1280]{1,0:T(8,128)(2,1)S(1)}, u32[]{:S(2)}, u32[]{:S(2)}) collective-permute-start(bf16[16,1280]{1,0:T(8,128)(2,1)S(1)} %slice_bitcast_fusion), channel_id=1, source_target_pairs={{0,1},{1,2},{2,3},{3,4},{4,5},{5,6},{6,7},{8,9},{9,10},{10,11},{11... | collective-permute-start | bytes 122888 | tf_op jit(solution)/shard_map/ppermute | solution.py:30
  3.8 0.8 collective-permute-done.rim_ref
  5.2 16.6 %conv.1 = (bf16[4096,1024]{1,0:T(8,128)(2,1)}, bf16[4096,128]{1,0:T(8,128)(2,1)}, bf16[4096,128]{1,0:T(8,128)(2,1)}, s32[16]{0:T(128)}) custom-call(s32[1]{0:T(128)} %bitcast.shard_ref, s32[1,32]{1,0:T(1,128)} %bounds.1, s32[1,32]{1,0:T(1,128)} %owners.1, bf16[4096,1280]{1,0:T(8,128)(2,1)} %bitcast.11, bf16[16,1280]{1,0:T(8,128)(2,1)} %copy-done.4, ...), custom_call_target="tpu_custom_call" | custom-call | flops 4194304000 | bytes 22020096 | tf_op jit(solution)/shard_map/conv/pallas_call | solution.py:532
  21.8 14.9 %states.1 = (f32[16,4096]{1,0:T(8,128)}, f32[16,4096]{1,0:T(8,128)}, bf16[32,128,1024]{2,1,0:T(8,128)(2,1)}, bf16[144,1024]{1,0:T(8,128)(2,1)}) custom-call(s32[16]{0:T(128)} %get-tuple-element.27.meta, bf16[4096,1024]{1,0:T(8,128)(2,1)} %get-tuple-element.28.act_ref.act_hbm, bf16[4096,128]{1,0:T(8,128)(2,1)} %get-tuple-element.29.b_ref.b_hbm, ...), custom_call_target="tpu_custom_call" | custom-call | flops 2147483648 | bytes 23068672 | tf_op jit(solution)/shard_map/states/pallas_call | solution.py:559
  36.7 2.7 %collective-permute-start.1 = (bf16[144,1024]{1,0:T(8,128)(2,1)}, bf16[144,1024]{1,0:T(8,128)(2,1)S(1)}, u32[]{:S(2)}, u32[]{:S(2)}) collective-permute-start(bf16[144,1024]{1,0:T(8,128)(2,1)} %get-tuple-element.30.own_ref), channel_id=1, source_target_pairs={{0,1},{1,0},{2,3},{3,2},{4,5},{5,4},{6,7},{7,6},{8,9},{9,8},{10,11... | collective-permute-start | bytes 884744 | tf_op jit(solution)/shard_map/ppermute | solution.py:620
  39.4 1.4 %collective-permute-done.1.got_ref.early_ref = bf16[144,1024]{1,0:T(8,128)(2,1)S(1)} collective-permute-done((bf16[144,1024]{1,0:T(8,128)(2,1)}, bf16[144,1024]{1,0:T(8,128)(2,1)S(1)}, u32[]{:S(2)}, u32[]{:S(2)}) %collective-permute-start.1) | collective-permute-done | bytes 294944 | tf_op jit(solution)/shard_map/ppermute | solution.py:620
  40.9 1.0 copy-done
  41.9 7.6 %finals.1 = (bf16[8,1056,128]{2,1,0:T(8,128)(2,1)}, f32[8,1024]{1,0:T(8,128)}) custom-call(s32[16]{0:T(128)} %get-tuple-element.27.meta, bf16[4096,1024]{1,0:T(8,128)(2,1)} %get-tuple-element.28.act_ref.act_hbm, bf16[4096,128]{1,0:T(8,128)(2,1)} %get-tuple-element.29.b_ref.b_hbm, bf16[32,128,1024]{2,1,0:T(8,128)(2,1)} %get-tuple-element.37.sin_hbm.sin_ref, ...), custom_call_target="tpu_custom_call" | custom-call | flops 268435456 | bytes 6291456 | tf_op jit(solution)/shard_map/finals/pallas_call | solution.py:632
  49.5 4.5 %all-to-all-start = ((bf16[4,2,1056,128]{3,2,1,0:T(8,128)(2,1)}), bf16[4,2,1056,128]{3,2,1,0:T(8,128)(2,1)}, u32[]{:S(2)}, u32[]{:S(2)}) async-start(bf16[4,2,1056,128]{3,2,1,0:T(8,128)(2,1)} %bitcast.17), calls=%async_computation | async-start | bytes 4325376 | tf_op jit(solution)/shard_map/all_to_all | solution.py:662
  54.0 3.9 %collective-permute-start.2 = (bf16[144,512]{1,0:T(8,128)(2,1)S(1)}, bf16[144,512]{1,0:T(8,128)(2,1)S(1)}, u32[]{:S(2)}, u32[]{:S(2)}) collective-permute-start(bf16[144,512]{1,0:T(8,128)(2,1)S(1)} %pair.1), channel_id=1, source_target_pairs={{0,6},{1,7},{8,14},{9,15},{16,22},{17,23},{24,30},{25,31}} | collective-permute-start | bytes 442376 | tf_op jit(solution)/shard_map/ppermute | solution.py:30
  57.9 1.3 %collective-permute-start.3 = (bf16[144,512]{1,0:T(8,128)(2,1)S(1)}, bf16[144,512]{1,0:T(8,128)(2,1)S(1)}, u32[]{:S(2)}, u32[]{:S(2)}) collective-permute-start(bf16[144,512]{1,0:T(8,128)(2,1)S(1)} %pair.1), channel_id=1, source_target_pairs={{0,4},{1,5},{2,6},{3,7},{8,12},{9,13},{10,14},{11,15},{16,20},{17,... | collective-permute-start | bytes 442376 | tf_op jit(solution)/shard_map/ppermute | solution.py:30
  59.2 2.5 %collective-permute-start.4 = (bf16[144,512]{1,0:T(8,128)(2,1)S(1)}, bf16[144,512]{1,0:T(8,128)(2,1)S(1)}, u32[]{:S(2)}, u32[]{:S(2)}) collective-permute-start(bf16[144,512]{1,0:T(8,128)(2,1)S(1)} %pair.1), channel_id=1, source_target_pairs={{0,2},{1,3},{2,4},{3,5},{4,6},{5,7},{8,10},{9,11},{10,12},{11,13},... | collective-permute-start | bytes 442376 | tf_op jit(solution)/shard_map/ppermute | solution.py:30
  61.7 21.5 %outputs.1.base_hbm = bf16[4096,1024]{1,0:T(8,128)(2,1)} custom-call(s32[16]{0:T(128)} %get-tuple-element.27.meta, bf16[4096,1024]{1,0:T(8,128)(2,1)} %get-tuple-element.28.act_ref.act_hbm, bf16[4096,128]{1,0:T(8,128)(2,1)} %get-tuple-element.29.b_ref.b_hbm, bf16[4096,128]{1,0:T(8,128)(2,1)} %get-tuple-element.31.c_ref, f32[16,4096]{1,0:T(8,128)} %bitcast.16, ...), custom_call_target="tpu_custom_call" | custom-call | flops 4294967296 | bytes 33554432 | tf_op jit(solution)/shard_map/outputs/pallas_call | solution.py:594
  83.5 1.3 %collective-permute-done.5.other_ref = bf16[128,512]{1,0:T(8,128)(2,1)S(1)} collective-permute-done((bf16[128,512]{1,0:T(8,128)(2,1)S(1)}, bf16[128,512]{1,0:T(8,128)(2,1)S(1)}, u32[]{:S(2)}, u32[]{:S(2)}) %collective-permute-start.5) | collective-permute-done | bytes 131104 | tf_op jit(solution)/shard_map/ppermute | solution.py:675
  84.8 0.8 carry.1
  85.6 0.7 copy-done.1
  86.3 3.2 %collective-permute-start.6 = (bf16[1024,128]{1,0:T(8,128)(2,1)S(1)}, bf16[1024,128]{1,0:T(8,128)(2,1)S(1)}, u32[]{:S(2)}, u32[]{:S(2)}) collective-permute-start(bf16[1024,128]{1,0:T(8,128)(2,1)S(1)} %get-tuple-element.47), channel_id=1, source_target_pairs={{0,24},{8,16},{16,8},{24,0},{1,25},{9,17},{17,9},{25,1},{2,26},{10... | collective-permute-start | bytes 786440 | tf_op jit(solution)/shard_map/ppermute | solution.py:689
  89.5 1.3 %collective-permute-start.7 = (bf16[1024,128]{1,0:T(8,128)(2,1)S(1)}, bf16[1024,128]{1,0:T(8,128)(2,1)S(1)}, u32[]{:S(2)}, u32[]{:S(2)}) collective-permute-start(bf16[1024,128]{1,0:T(8,128)(2,1)S(1)} %get-tuple-element.48), channel_id=1, source_target_pairs={{0,16},{8,24},{16,0},{24,8},{1,17},{9,25},{17,1},{25,9},{2,18},{10... | collective-permute-start | bytes 786440 | tf_op jit(solution)/shard_map/ppermute | solution.py:689
  90.8 0.9 slice.15
  92.3 1.5 %correct.1 = bf16[4096,1024]{1,0:T(8,128)(2,1)} custom-call(s32[16]{0:T(128)} %get-tuple-element.27.meta, bf16[4096,1024]{1,0:T(8,128)(2,1)} %outputs.1.base_hbm, bf16[4096,128]{1,0:T(8,128)(2,1)} %get-tuple-element.31.c_ref, f32[16,4096]{1,0:T(8,128)} %get-tuple-element.35.carry_ref, bf16[128,1024]{1,0:T(8,128)(2,1)} %copy-done.1, ...), custom_call_target="tpu_custom_call", output_to_operand_aliasing={{}: (1, {})} | custom-call | flops 1073741824 | bytes 18874368 | tf_op jit(solution)/shard_map/correct/pallas_call | solution.py:691
  93.9 2.8 %collective-permute-done.6 = bf16[1024,128]{1,0:T(8,128)(2,1)S(1)} collective-permute-done((bf16[1024,128]{1,0:T(8,128)(2,1)S(1)}, bf16[1024,128]{1,0:T(8,128)(2,1)S(1)}, u32[]{:S(2)}, u32[]{:S(2)}) %collective-permute-start.6) | collective-permute-done | bytes 262176 | tf_op jit(solution)/shard_map/ppermute | solution.py:689
  96.7 5.3 %collective-permute-done.7 = bf16[1024,128]{1,0:T(8,128)(2,1)S(1)} collective-permute-done((bf16[1024,128]{1,0:T(8,128)(2,1)S(1)}, bf16[1024,128]{1,0:T(8,128)(2,1)S(1)}, u32[]{:S(2)}, u32[]{:S(2)}) %collective-permute-start.7) | collective-permute-done | bytes 262176 | tf_op jit(solution)/shard_map/ppermute | solution.py:689
  102.2 4.2 %convert_add_fusion = f32[4,2,1024,128]{3,2,1,0:T(8,128)} fusion(bf16[4,2,1056,128]{3,2,1,0:T(8,128)(2,1)} %all-to-all-done, pred[2]{0:T(512)(128)(4,1)S(1)} %iota_compare_fusion, bf16[4,1024,128]{2,1,0:T(8,128)(2,1)S(1)} %select_select_fusion), kind=kLoop, calls=%fused_computation | loop fusion | flops 4194304 | bytes 7340034 | tf_op jit(solution)/shard_map/add | solution.py:715
  (23 shorter events, 1.9 us)
Async XLA Ops:
  1.4 3.2 %collective-permute-start = (bf16[16,1280]{1,0:T(8,128)(2,1)S(1)}, bf16[16,1280]{1,0:T(8,128)(2,1)S(1)}, u32[]{:S(2)}, u32[]{:S(2)}) collective-permute-start(bf16[16,1280]{1,0:T(8,128)(2,1)S(1)} %slice_bitcast_fusion), channel_id=1, source_target_pairs={{0,1},{1,2},{2,3},{3,4},{4,5},{5,6},{6,7},{8,9},{9,10},{10,11},{11... | collective-permute-start | bytes 122888 | tf_op jit(solution)/shard_map/ppermute | solution.py:30
  4.6 0.6 copy-start.4
  36.7 4.1 %collective-permute-start.1 = (bf16[144,1024]{1,0:T(8,128)(2,1)}, bf16[144,1024]{1,0:T(8,128)(2,1)S(1)}, u32[]{:S(2)}, u32[]{:S(2)}) collective-permute-start(bf16[144,1024]{1,0:T(8,128)(2,1)} %get-tuple-element.30.own_ref), channel_id=1, source_target_pairs={{0,1},{1,0},{2,3},{3,2},{4,5},{5,4},{6,7},{7,6},{8,9},{9,8},{10,11... | collective-permute-start | bytes 884744 | tf_op jit(solution)/shard_map/ppermute | solution.py:620
  40.9 1.0 copy-start
  49.5 35.2 %all-to-all-start = ((bf16[4,2,1056,128]{3,2,1,0:T(8,128)(2,1)}), bf16[4,2,1056,128]{3,2,1,0:T(8,128)(2,1)}, u32[]{:S(2)}, u32[]{:S(2)}) async-start(bf16[4,2,1056,128]{3,2,1,0:T(8,128)(2,1)} %bitcast.17), calls=%async_computation | async-start | bytes 4325376 | tf_op jit(solution)/shard_map/all_to_all | solution.py:662
  54.0 29.2 %collective-permute-start.2 = (bf16[144,512]{1,0:T(8,128)(2,1)S(1)}, bf16[144,512]{1,0:T(8,128)(2,1)S(1)}, u32[]{:S(2)}, u32[]{:S(2)}) collective-permute-start(bf16[144,512]{1,0:T(8,128)(2,1)S(1)} %pair.1), channel_id=1, source_target_pairs={{0,6},{1,7},{8,14},{9,15},{16,22},{17,23},{24,30},{25,31}} | collective-permute-start | bytes 442376 | tf_op jit(solution)/shard_map/ppermute | solution.py:30
  57.9 25.4 %collective-permute-start.3 = (bf16[144,512]{1,0:T(8,128)(2,1)S(1)}, bf16[144,512]{1,0:T(8,128)(2,1)S(1)}, u32[]{:S(2)}, u32[]{:S(2)}) collective-permute-start(bf16[144,512]{1,0:T(8,128)(2,1)S(1)} %pair.1), channel_id=1, source_target_pairs={{0,4},{1,5},{2,6},{3,7},{8,12},{9,13},{10,14},{11,15},{16,20},{17,... | collective-permute-start | bytes 442376 | tf_op jit(solution)/shard_map/ppermute | solution.py:30
  59.2 24.1 %collective-permute-start.4 = (bf16[144,512]{1,0:T(8,128)(2,1)S(1)}, bf16[144,512]{1,0:T(8,128)(2,1)S(1)}, u32[]{:S(2)}, u32[]{:S(2)}) collective-permute-start(bf16[144,512]{1,0:T(8,128)(2,1)S(1)} %pair.1), channel_id=1, source_target_pairs={{0,2},{1,3},{2,4},{3,5},{4,6},{5,7},{8,10},{9,11},{10,12},{11,13},... | collective-permute-start | bytes 442376 | tf_op jit(solution)/shard_map/ppermute | solution.py:30
  61.7 23.1 %copy-start.2 = (f32[8,1024]{1,0:T(8,128)S(1)}, f32[8,1024]{1,0:T(8,128)}, u32[]{:S(2)}) copy-start(f32[8,1024]{1,0:T(8,128)} %get-tuple-element.44.first_ref) | copy-start | bytes 98308
  61.7 23.1 %copy-start.3 = (s32[16]{0:T(128)S(1)}, s32[16]{0:T(128)}, u32[]{:S(2)}) copy-start(s32[16]{0:T(128)} %get-tuple-element.27.meta) | copy-start | bytes 196
  83.3 1.4 %collective-permute-start.5 = (bf16[128,512]{1,0:T(8,128)(2,1)S(1)}, bf16[128,512]{1,0:T(8,128)(2,1)S(1)}, u32[]{:S(2)}, u32[]{:S(2)}) collective-permute-start(bf16[128,512]{1,0:T(8,128)(2,1)S(1)} %prefix.1.mine_ref), channel_id=1, source_target_pairs={{0,1},{1,0},{2,3},{3,2},{4,5},{5,4},{6,7},{7,6},{8,9},{9,8},{10,11... | collective-permute-start | bytes 393224 | tf_op jit(solution)/shard_map/ppermute | solution.py:675
  85.6 0.7 copy-start.1
  86.3 10.4 %collective-permute-start.6 = (bf16[1024,128]{1,0:T(8,128)(2,1)S(1)}, bf16[1024,128]{1,0:T(8,128)(2,1)S(1)}, u32[]{:S(2)}, u32[]{:S(2)}) collective-permute-start(bf16[1024,128]{1,0:T(8,128)(2,1)S(1)} %get-tuple-element.47), channel_id=1, source_target_pairs={{0,24},{8,16},{16,8},{24,0},{1,25},{9,17},{17,9},{25,1},{2,26},{10... | collective-permute-start | bytes 786440 | tf_op jit(solution)/shard_map/ppermute | solution.py:689
  89.5 12.5 %collective-permute-start.7 = (bf16[1024,128]{1,0:T(8,128)(2,1)S(1)}, bf16[1024,128]{1,0:T(8,128)(2,1)S(1)}, u32[]{:S(2)}, u32[]{:S(2)}) collective-permute-start(bf16[1024,128]{1,0:T(8,128)(2,1)S(1)} %get-tuple-element.48), channel_id=1, source_target_pairs={{0,16},{8,24},{16,0},{24,8},{1,17},{9,25},{17,1},{25,9},{2,18},{10... | collective-permute-start | bytes 786440 | tf_op jit(solution)/shard_map/ppermute | solution.py:689
  90.7 11.2 %collective-permute-start.8 = (bf16[1024,128]{1,0:T(8,128)(2,1)S(1)}, bf16[1024,128]{1,0:T(8,128)(2,1)S(1)}, u32[]{:S(2)}, u32[]{:S(2)}) collective-permute-start(bf16[1024,128]{1,0:T(8,128)(2,1)S(1)} %get-tuple-element.49), channel_id=1, source_target_pairs={{0,8},{8,0},{16,24},{24,16},{1,9},{9,1},{17,25},{25,17},{2,10},{10... | collective-permute-start | bytes 786440 | tf_op jit(solution)/shard_map/ppermute | solution.py:689
where the time goes:
time: 108 us; the launch traced here: 106 us
  Pallas kernels  63.1 us (58%)
  starting transfers between devices  21.8 us (20%)
  waiting for transfers between devices  11.7 us (11%)
  local copies, waits for them, and re-layouts  4.63 us (4%)
  other arithmetic  4.45 us (4%)
    pallas_call x1, Pallas kernels, outputs(): pl.pallas_call(functools.partial(output_kernel, first, bool(late)), grid_...  21.5 us
    pallas_call x1, Pallas kernels, on_device(): pl.pallas_call(conv_kernel, grid=(steps,), in_specs=[smem, smem, smem, by...  16.6 us
    pallas_call x1, Pallas kernels, on_device(): pl.pallas_call(states_kernel, grid_spec=prefetch(grid=(steps,), in_specs=...  14.9 us
    ppermute x4, starting transfers between devices, shifted(): lax.ppermute(value, axis, [(source, source + steps) for source in range(l...  9.98 us
    ppermute x3, waiting for transfers between devices, on_device(): more.append(lax.ppermute(send[apart], 'stream', swap))  8.11 us
    pallas_call x1, Pallas kernels, on_device(): pl.pallas_call(finals_kernel, in_specs=[smem, in_hbm, in_hbm, in_hbm, in_...  7.61 us
    all_to_all x1, starting transfers between devices, on_device(): lax.all_to_all(fin.reshape(owners, CAP, rows, N), 'stream', split_axis=0,...  4.49 us
    ppermute x3, starting transfers between devices, on_device(): more.append(lax.ppermute(send[apart], 'stream', swap))  4.47 us
  transfers between devices with their start and end apart: 10, of which 5 were waited for; matrix products, arithmetic and copies ran while one was open for 1% of the time, Pallas kernels for 22%

commit v1 on v0

--- a/solution.py
+++ b/solution.py
@@ -106,12 +106,15 @@
     meta[0] = start - anchor
 
 
-def conv_kernel(
+def states_kernel(
     shard_ref, bounds, owners, x_ref, rim_ref, w_ref, bias_ref, move_ref, slot_ref,
-    act_ref, b_ref, c_ref, meta,
-    edge16, weights, moves, count,
+    dt_ref, ld_ref, rep_ref, rep16_ref, tri_ref,
+    act_ref, b_ref, c_ref, cum_ref, carry_ref, sin_ref, pay_ref, meta,
+    edge16, weights, moves, state, total, count,
 ):
     step = pl.program_id(0)
+    heads = dt_ref.shape[0]
+    width = rep_ref.shape[1]
     span = pl.num_programs(0) * BLOCK
     parts = BLOCK // CHUNK
     first = step * BLOCK
@@ -123,6 +126,8 @@
         weights[0:4] = 0.5 * w_ref[...]
         weights[4:5] = 0.5 * bias_ref[...].reshape(1, weights.shape[1])
         moves[0] = move_ref[...]
+        state[...] = jnp.zeros_like(state)
+        total[...] = jnp.zeros_like(total)
 
     choices = []
     for part in range(parts):
@@ -164,30 +169,12 @@
 
     edge16[...] = x_ref[BLOCK - 16 :, :]
 
-
-def states_kernel(
-    meta, act_ref, b_ref, dt_ref, ld_ref, rep_ref, rep16_ref, tri_ref,
-    cum_ref, carry_ref, sin_ref, pay_ref,
-    state, total,
-):
-    step = pl.program_id(0)
-    heads = dt_ref.shape[0]
-    width = rep_ref.shape[1]
-    span = pl.num_programs(0) * BLOCK
-    parts = BLOCK // CHUNK
-    first = step * BLOCK
-
-    @pl.when(step == 0)
-    def _():
-        state[...] = jnp.zeros_like(state)
-        total[...] = jnp.zeros_like(total)
-
     spans = [slice(part * CHUNK, part * CHUNK + CHUNK) for part in range(parts)]
     pieces = jnp.concatenate([thirds(ld_ref[:, rows] * LOG2E) for rows in spans], axis=0)
     summed = jnp.dot(pieces, tri_ref[...], preferred_element_type=F32)
     open_end = jnp.where(meta[0] < 0, meta[1], -1)
     running = total[...]
-    weights = []
+    scales = []
     throughs = []
     for part, rows in enumerate(spans):
         begin = first + part * CHUNK
@@ -199,11 +186,11 @@
         start = last_start(meta, begin + CHUNK - 1)
         last = cum[:, CHUNK - 1 :]
         weight = jnp.where(lane >= start, jnp.exp2(last - cum) * dt_ref[:, rows], 0.0)
-        weights.append(weight.T.astype(BF16))
+        scales.append(weight.T.astype(BF16))
         throughs.append(spread_row(jnp.where(start < begin, jnp.exp2(last), 0.0), rep_ref[...]))
         running = running + last
     total[...] = running
-    weight = jnp.concatenate(weights, axis=0)
+    weight = jnp.concatenate(scales, axis=0)
     turned = [b_ref[rows, :].T for rows in spans]
     for tile in range(width // 256):
         cols = slice(tile * 256, tile * 256 + 256)
@@ -235,7 +222,7 @@
     width = rep_ref.shape[1]
 
     def place(slot):
-        return pl.multiple_of((meta[1 + slot] - 1) // CHUNK * CHUNK, CHUNK)
+        return pl.multiple_of((jnp.minimum(meta[1 + slot], span) - 1) // CHUNK * CHUNK, CHUNK)
 
     def copies(slot):
         low = place(slot)
@@ -250,15 +237,9 @@
             for index, (source, target) in enumerate(pairs)
         ]
 
-    def fetch(slot, _):
-        for copy in copies(slot):
-            copy.start()
-        return 0
-
-    found = jnp.int32(0)
-    for slot in range(EMAX):
-        found = found + (meta[1 + slot] <= span).astype(jnp.int32)
-    lax.fori_loop(0, found, fetch, 0)
+    fetched = [copies(slot) for slot in range(EMAX)]
+    for copy in sum(fetched, []):
+        copy.start()
     blank[...] = jnp.zeros_like(blank)
     blanks = [
         pltpu.make_async_copy(blank, fin_hbm.at[index], blank_sem.at[index])
@@ -266,16 +247,12 @@
     ]
     for copy in blanks:
         copy.start()
-    first_ref[...] = jnp.zeros_like(first_ref)
     lines[...] = jnp.zeros_like(lines)
-    for copy in blanks:
+    for copy in sum(fetched, []):
         copy.wait()
-
-    def finish(slot, _):
-        for copy in copies(slot):
-            copy.wait()
+    for slot in range(EMAX):
         end = meta[1 + slot]
-        start = jnp.where(slot > 0, meta[jnp.maximum(slot, 1)], meta[0])
+        start = meta[slot]
         low = place(slot)
         there = pl.ds(low, CHUNK)
         lane = iota((heads, CHUNK), 1) + low
@@ -289,13 +266,9 @@
         local = outer_dot(b_held[slot], load)
         through = spread_row(jnp.where(start < low, jnp.exp2(at_end), 0.0), rep_ref[...])
         final = local + through * sin_held[slot].astype(F32)
-        target = meta[5 + slot]
-
-        @pl.when((slot == 0) & (start < 0))
-        def _():
+        if slot == 0:
             opened = jnp.sum(jnp.where(lane == end - 1, carry_ref[:, there], 0.0), axis=1, keepdims=True)
             first_ref[...] = jnp.broadcast_to(spread_row(opened, rep_ref[...]), first_ref.shape)
-
         row = iota((16, CHUNK), 0)
         col = iota((16, CHUNK), 1) + low
         pick = (col == end - 3 + row) & (col >= start) & (row < 3)
@@ -310,29 +283,31 @@
         for index in range(3):
             for tile in range(tiles):
                 at = index * tiles + tile
-                lines[at : at + 1] = last[index : index + 1, tile * 128 : tile * 128 + 128]
-
-        @pl.when(target >= 0)
+                lines[slot, at : at + 1] = last[index : index + 1, tile * 128 : tile * 128 + 128]
+
+        made[slot, :width] = final.astype(BF16).T
+        made[slot, width:] = lines[slot].astype(BF16)
+    for copy in blanks:
+        copy.wait()
+    used = [(meta[1 + slot] <= span) & (meta[5 + slot] >= 0) for slot in range(EMAX)]
+
+    def send(slot):
+        return pltpu.make_async_copy(made.at[slot], fin_hbm.at[meta[5 + slot]], made_sem.at[slot])
+
+    for slot in range(EMAX):
+
+        @pl.when(used[slot])
         def _():
-            made[slot, :width] = final.astype(BF16).T
-            made[slot, width:] = lines[...].astype(BF16)
-            pltpu.make_async_copy(made.at[slot], fin_hbm.at[target], made_sem.at[slot]).start()
-
-        return 0
-
-    lax.fori_loop(0, found, finish, 0)
-
-    def close(slot, _):
-        @pl.when(meta[5 + slot] >= 0)
+            send(slot).start()
+
+    for slot in range(EMAX):
+
+        @pl.when(used[slot])
         def _():
-            pltpu.make_async_copy(made.at[slot], fin_hbm.at[meta[5 + slot]], made_sem.at[slot]).wait()
-
-        return 0
-
-    lax.fori_loop(0, found, close, 0)
-
-
-def output_kernel(origin, late, meta, act_ref, b_ref, c_ref, dt_ref, cum_ref, sin_ref, gain_in, rep_ref, rep16_ref, each_ref, *refs):
+            send(slot).wait()
+
+
+def output_kernel(origin, late, meta, act_ref, b_ref, c_ref, dt_ref, cum_ref, sin_ref, gain_in, rep_ref, rep16_ref, *refs):
     out_ref, gain_ref = refs[-2:]
     step = origin + pl.program_id(0)
     heads = dt_ref.shape[0]
@@ -351,18 +326,13 @@
         rows = slice(part * CHUNK, part * CHUNK + CHUNK)
         cum = cum_ref[:, rows]
         back = cum - jnp.log2(dt_ref[:, rows])
-        ahead = jnp.concatenate(
-            [thirds(cum), jnp.ones((3 * heads, CHUNK), BF16), jnp.zeros((CHUNK - 6 * heads, CHUNK), BF16)], axis=0
-        ).T
-        back = thirds(-back)
+        ahead = cum.T
         b_act = b_ref[rows, :]
         c_act = c_ref[rows, :]
         place = iota((CHUNK, CHUNK), 0) + begin
         other = iota((CHUNK, CHUNK), 1) + begin
         scores = lax.dot_general(c_act, b_act, (((1,), (1,)), ((), ())), preferred_element_type=F32)
         scores = jnp.where((other <= place) & (other >= starts_of(meta, place)), scores, 0.0)
-        scores = jnp.concatenate([scores, scores], axis=1)
-        blank = jnp.zeros((CHUNK - 6 * heads, 256), BF16)
         lane = iota((heads, CHUNK), 1) + begin
         before = jnp.where(last_start(meta, begin) < begin, next_end(meta, begin), -1)
         entry = jnp.where(lane < before, jnp.exp2(cum), 0.0)
@@ -377,10 +347,11 @@
             scale = jnp.dot(entry, rep16_ref[:, cols], preferred_element_type=F32)
             sums = []
             for pair in (2 * quad, 2 * quad + 1):
-                own = each_ref[:, pair * 256 : pair * 256 + 256]
-                against = jnp.concatenate([own, jnp.concatenate([back, back], axis=1) * own, blank], axis=0)
-                spread = jnp.dot(ahead, against, preferred_element_type=F32)
-                mix = (jnp.exp2(jnp.minimum(spread, 0.0)) * scores).astype(BF16)
+                mixes = []
+                for head in (2 * pair, 2 * pair + 1):
+                    spread = jnp.minimum(ahead[:, head : head + 1] - back[head : head + 1, :], 0.0)
+                    mixes.append((jnp.exp2(spread) * scores).astype(BF16))
+                mix = jnp.concatenate(mixes, axis=1)
                 x_pair = act_ref[rows, pair * 128 : pair * 128 + 128]
                 zero = jnp.zeros_like(x_pair)
                 split = jnp.concatenate(
@@ -513,8 +484,6 @@
     rim = shifted(rows_in[span - 16 :], "seq", 1)
     rep = (np.arange(width)[None, :] // P_SIZE == np.arange(heads)[:, None]).astype(np.float32)
     rep16 = np.concatenate([rep, rep], 0).astype(BF16)
-    each = np.arange(heads * CHUNK)[None, :] // CHUNK == np.arange(3 * heads)[:, None] % heads
-    each = each.astype(BF16)
     ticks = np.arange(CHUNK)
     tri = (ticks[:, None] <= ticks[None, :]).astype(BF16)
     order = np.arange(3 * CHUNK)
@@ -529,64 +498,47 @@
     by_rows = pl.BlockSpec((BLOCK, channels), lambda i, *_: (i, 0))
     by_width = pl.BlockSpec((BLOCK, width), lambda i, *_: (i, 0))
     by_rest = pl.BlockSpec((BLOCK, N), lambda i, *_: (i, 0))
-    act, b_act, c_act, meta = pl.pallas_call(
-        conv_kernel,
+    in_hbm = pl.BlockSpec(memory_space=pl.ANY)
+    act, b_act, c_act, cum, carry, sin, pay, meta = pl.pallas_call(
+        states_kernel,
         grid=(steps,),
         in_specs=[
             smem, smem, smem, by_rows, whole((16, channels)),
             whole((4, channels)), whole((channels,)), whole(move.shape), whole(slot.shape),
-        ],
-        out_specs=[by_width, by_rest, by_rest, smem],
+            per_head, per_head, whole((heads, width)), whole((2 * heads, width)), whole((CHUNK, CHUNK)),
+        ],
+        out_specs=[
+            by_width, by_rest, by_rest, per_head, per_head,
+            pl.BlockSpec((BLOCK // CHUNK, N, width), lambda i, *_: (i, 0, 0)),
+            whole((PAY, width)), smem,
+        ],
         out_shape=[
             jax.ShapeDtypeStruct((span, width), BF16),
             jax.ShapeDtypeStruct((span, N), BF16),
             jax.ShapeDtypeStruct((span, N), BF16),
+            jax.ShapeDtypeStruct((heads, span), F32),
+            jax.ShapeDtypeStruct((heads, span), F32),
+            jax.ShapeDtypeStruct((chunks, N, width), BF16),
+            jax.ShapeDtypeStruct((PAY, width), BF16),
             jax.ShapeDtypeStruct((16,), jnp.int32),
         ],
         scratch_shapes=[
             pltpu.VMEM((16, channels), BF16),
             pltpu.VMEM((8, channels), F32),
             pltpu.VMEM((1 + BLOCK // CHUNK,) + move.shape, BF16),
+            pltpu.VMEM((N, width), F32),
+            pltpu.VMEM((heads, CHUNK), F32),
             pltpu.SMEM((owners,), jnp.int32),
         ],
         compiler_params=params(60),
         cost_estimate=pl.CostEstimate(
-            flops=2 * span * channels * 400, bytes_accessed=21 << 20, transcendentals=span * channels
-        ),
-        name="conv",
-    )(shard, doc_bounds, doc_owner, rows_in, rim, conv_weight, conv_bias, move, slot)
-    in_hbm = pl.BlockSpec(memory_space=pl.ANY)
-    cum, carry, sin, pay = pl.pallas_call(
-        states_kernel,
-        grid_spec=prefetch(
-            grid=(steps,),
-            in_specs=[
-                by_width, by_rest, per_head, per_head,
-                whole((heads, width)), whole((2 * heads, width)), whole((CHUNK, CHUNK)),
-            ],
-            out_specs=[
-                per_head, per_head,
-                pl.BlockSpec((BLOCK // CHUNK, N, width), lambda i, *_: (i, 0, 0)),
-                whole((PAY, width)),
-            ],
-            scratch_shapes=[
-                pltpu.VMEM((N, width), F32),
-                pltpu.VMEM((heads, CHUNK), F32),
-            ],
-        ),
-        out_shape=[
-            jax.ShapeDtypeStruct((heads, span), F32),
-            jax.ShapeDtypeStruct((heads, span), F32),
-            jax.ShapeDtypeStruct((chunks, N, width), BF16),
-            jax.ShapeDtypeStruct((PAY, width), BF16),
-        ],
-        compiler_params=params(60),
-        cost_estimate=pl.CostEstimate(
-            flops=2 * span * width * N * 2, bytes_accessed=22 << 20, transcendentals=span * heads
+            flops=2 * span * channels * 600, bytes_accessed=32 << 20, transcendentals=span * channels
         ),
         name="states",
-    )(meta, act, b_act, step_size[0], log_decay[0], rep, rep16, tri)
-
+    )(
+        shard, doc_bounds, doc_owner, rows_in, rim, conv_weight, conv_bias, move, slot,
+        step_size[0], log_decay[0], rep, rep16, tri,
+    )
 
     def outputs(first, last, late=()):
         rows_of = functools.partial(pl.BlockSpec, index_map=lambda i, *_: (first + i, 0))
@@ -598,7 +550,7 @@
                 in_specs=[
                     rows_of((BLOCK, width)), rows_of((BLOCK, N)), rows_of((BLOCK, N)), heads_of, heads_of,
                     pl.BlockSpec((BLOCK // CHUNK, N, width), lambda i, *_: (first + i, 0, 0)),
-                    smem, whole((heads, width)), whole((2 * heads, width)), whole(each.shape),
+                    smem, whole((heads, width)), whole((2 * heads, width)),
                 ] + ([heads_of, whole((N, width)), pl.BlockSpec(memory_space=pl.ANY)] if late else []),
                 out_specs=rows_of((BLOCK, width)),
                 scratch_shapes=[pltpu.VMEM((1, width), F32)],
@@ -612,7 +564,7 @@
                 transcendentals=(last - first) * BLOCK * CHUNK * heads,
             ),
             name="outputs",
-        )(meta, act, b_act, c_act, step_size[0], cum, sin, skip_gain, rep, rep16, each, *late)
+        )(meta, act, b_act, c_act, step_size[0], cum, sin, skip_gain, rep, rep16, *late)
 
     side = width // 2
     count = lax.axis_size("seq")
@@ -649,7 +601,7 @@
             pltpu.VMEM((EMAX, 16, channels), BF16),
             pltpu.VMEM((rows, N), BF16),
             pltpu.VMEM((EMAX, rows, N), BF16),
-            pltpu.VMEM((TAIL, N), F32),
+            pltpu.VMEM((EMAX, TAIL, N), F32),
             pltpu.SemaphoreType.DMA((EMAX, 5)),
             pltpu.SemaphoreType.DMA((slots,)),
             pltpu.SemaphoreType.DMA((EMAX,)),

time: 108 us -> 102 us (0.944)
  Pallas kernels: 63.1 us -> 55.3 us
  starting transfers between devices: 21.8 us -> 23.1 us
    pallas_call x2 -> x1, Pallas kernels: 31.5 us -> 25 us  [on_device(): pl.pallas_call(states_kernel, grid=(steps,), in_specs=[smem, smem, smem,...]
  transfers between devices with their start and end apart: 10 -> 10, of which waited for: 5 -> 6; matrix products, arithmetic and copies ran while one was open for 1% -> 2% of each run, Pallas kernels for 22% -> 22%
where the time goes in v1:
time: 102 us; the launch traced here: 101 us
  Pallas kernels  55.3 us (54%)
  starting transfers between devices  23.1 us (23%)
  waiting for transfers between devices  12.3 us (12%)
  local copies, waits for them, and re-layouts  4.63 us (5%)
  other arithmetic  4.45 us (4%)
    pallas_call x1, Pallas kernels, on_device(): pl.pallas_call(states_kernel, grid=(steps,), in_specs=[smem, smem, smem,...  25 us
    pallas_call x1, Pallas kernels, outputs(): pl.pallas_call(functools.partial(output_kernel, first, bool(late)), grid_...  20.8 us
    ppermute x4, starting transfers between devices, shifted(): lax.ppermute(value, axis, [(source, source + steps) for source in range(l...  10.9 us
    ppermute x3, waiting for transfers between devices, on_device(): more.append(lax.ppermute(send[apart], 'stream', swap))  8.94 us
    pallas_call x1, Pallas kernels, on_device(): pl.pallas_call(finals_kernel, in_specs=[smem, in_hbm, in_hbm, in_hbm, in_...  7 us
    all_to_all x1, starting transfers between devices, on_device(): lax.all_to_all(fin.reshape(owners, CAP, rows, N), 'stream', split_axis=0,...  4.47 us
    add x1, other arithmetic, on_device(): ssm = got[:, :, :width].astype(F32) + extra.astype(F32)  4.18 us
    ppermute x3, starting transfers between devices, on_device(): more.append(lax.ppermute(send[apart], 'stream', swap))  3.93 us
  transfers between devices with their start and end apart: 10, of which 6 were waited for; matrix products, arithmetic and copies ran while one was open for 2% of the time, Pallas kernels for 22%

profile of v1, /device:TPU:0, one launch (start us, length us, event | category | flops | bytes accessed | tf_op | source)
XLA Modules:
  0.0 100.6 jit_solution(1498379207249354015)
XLA Ops:
  0.6 0.8 slice_bitcast_fusion
  1.4 2.3 %collective-permute-start = (bf16[16,1280]{1,0:T(8,128)(2,1)S(1)}, bf16[16,1280]{1,0:T(8,128)(2,1)S(1)}, u32[]{:S(2)}, u32[]{:S(2)}) collective-permute-start(bf16[16,1280]{1,0:T(8,128)(2,1)S(1)} %slice_bitcast_fusion), channel_id=1, source_target_pairs={{0,1},{1,2},{2,3},{3,4},{4,5},{5,6},{6,7},{8,9},{9,10},{10,11},{11... | collective-permute-start | bytes 122888 | tf_op jit(solution)/shard_map/ppermute | solution.py:30
  3.8 0.8 collective-permute-done.rim_ref
  5.2 25.0 %states.1 = (bf16[4096,1024]{1,0:T(8,128)(2,1)}, bf16[4096,128]{1,0:T(8,128)(2,1)}, bf16[4096,128]{1,0:T(8,128)(2,1)}, f32[16,4096]{1,0:T(8,128)}, f32[16,4096]{...) custom-call(s32[1]{0:T(128)} %bitcast.shard_ref, s32[1,32]{1,0:T(1,128)} %bounds.1, ...), custom_call_target="tpu_custom_call" | custom-call | flops 6291456000 | bytes 33554432 | tf_op jit(solution)/shard_map/states/pallas_call | solution.py:502
  30.2 3.5 %collective-permute-start.1 = (bf16[144,1024]{1,0:T(8,128)(2,1)}, bf16[144,1024]{1,0:T(8,128)(2,1)S(1)}, u32[]{:S(2)}, u32[]{:S(2)}) collective-permute-start(bf16[144,1024]{1,0:T(8,128)(2,1)} %get-tuple-element.28.own_ref), channel_id=1, source_target_pairs={{0,1},{1,0},{2,3},{3,2},{4,5},{5,4},{6,7},{7,6},{8,9},{9,8},{10,11... | collective-permute-start | bytes 884744 | tf_op jit(solution)/shard_map/ppermute | solution.py:572
  33.7 1.4 %collective-permute-done.1.got_ref.early_ref = bf16[144,1024]{1,0:T(8,128)(2,1)S(1)} collective-permute-done((bf16[144,1024]{1,0:T(8,128)(2,1)}, bf16[144,1024]{1,0:T(8,128)(2,1)S(1)}, u32[]{:S(2)}, u32[]{:S(2)}) %collective-permute-start.1) | collective-permute-done | bytes 294944 | tf_op jit(solution)/shard_map/ppermute | solution.py:572
  35.1 1.0 copy-done
  36.2 7.0 %finals.1 = (bf16[8,1056,128]{2,1,0:T(8,128)(2,1)}, f32[8,1024]{1,0:T(8,128)}) custom-call(s32[16]{0:T(128)} %get-tuple-element.27.meta, bf16[4096,1024]{1,0:T(8,128)(2,1)} %get-tuple-element.29.act_hbm.act_ref, bf16[4096,128]{1,0:T(8,128)(2,1)} %get-tuple-element.30.b_hbm.b_ref, bf16[32,128,1024]{2,1,0:T(8,128)(2,1)} %get-tuple-element.37.sin_hbm.sin_ref, ...), custom_call_target="tpu_custom_call" | custom-call | flops 268435456 | bytes 6291456 | tf_op jit(solution)/shard_map/finals/pallas_call | solution.py:584
  43.2 4.5 %all-to-all-start = ((bf16[4,2,1056,128]{3,2,1,0:T(8,128)(2,1)}), bf16[4,2,1056,128]{3,2,1,0:T(8,128)(2,1)}, u32[]{:S(2)}, u32[]{:S(2)}) async-start(bf16[4,2,1056,128]{3,2,1,0:T(8,128)(2,1)} %bitcast.14), calls=%async_computation | async-start | bytes 4325376 | tf_op jit(solution)/shard_map/all_to_all | solution.py:614
  47.7 4.8 %collective-permute-start.2 = (bf16[144,512]{1,0:T(8,128)(2,1)S(1)}, bf16[144,512]{1,0:T(8,128)(2,1)S(1)}, u32[]{:S(2)}, u32[]{:S(2)}) collective-permute-start(bf16[144,512]{1,0:T(8,128)(2,1)S(1)} %pair.1), channel_id=1, source_target_pairs={{0,6},{1,7},{8,14},{9,15},{16,22},{17,23},{24,30},{25,31}} | collective-permute-start | bytes 442376 | tf_op jit(solution)/shard_map/ppermute | solution.py:30
  52.5 1.3 %collective-permute-start.3 = (bf16[144,512]{1,0:T(8,128)(2,1)S(1)}, bf16[144,512]{1,0:T(8,128)(2,1)S(1)}, u32[]{:S(2)}, u32[]{:S(2)}) collective-permute-start(bf16[144,512]{1,0:T(8,128)(2,1)S(1)} %pair.1), channel_id=1, source_target_pairs={{0,4},{1,5},{2,6},{3,7},{8,12},{9,13},{10,14},{11,15},{16,20},{17,... | collective-permute-start | bytes 442376 | tf_op jit(solution)/shard_map/ppermute | solution.py:30
  53.8 2.5 %collective-permute-start.4 = (bf16[144,512]{1,0:T(8,128)(2,1)S(1)}, bf16[144,512]{1,0:T(8,128)(2,1)S(1)}, u32[]{:S(2)}, u32[]{:S(2)}) collective-permute-start(bf16[144,512]{1,0:T(8,128)(2,1)S(1)} %pair.1), channel_id=1, source_target_pairs={{0,2},{1,3},{2,4},{3,5},{4,6},{5,7},{8,10},{9,11},{10,12},{11,13},... | collective-permute-start | bytes 442376 | tf_op jit(solution)/shard_map/ppermute | solution.py:30
  56.3 20.8 %outputs.1.base_hbm = bf16[4096,1024]{1,0:T(8,128)(2,1)} custom-call(s32[16]{0:T(128)} %get-tuple-element.27.meta, bf16[4096,1024]{1,0:T(8,128)(2,1)} %get-tuple-element.29.act_hbm.act_ref, bf16[4096,128]{1,0:T(8,128)(2,1)} %get-tuple-element.30.b_hbm.b_ref, bf16[4096,128]{1,0:T(8,128)(2,1)} %get-tuple-element.31.c_ref, f32[16,4096]{1,0:T(8,128)} %bitcast.17, ...), custom_call_target="tpu_custom_call" | custom-call | flops 4294967296 | bytes 33554432 | tf_op jit(solution)/shard_map/outputs/pallas_call | solution.py:546
  77.6 1.1 %collective-permute-done.5.other_ref = bf16[128,512]{1,0:T(8,128)(2,1)S(1)} collective-permute-done((bf16[128,512]{1,0:T(8,128)(2,1)S(1)}, bf16[128,512]{1,0:T(8,128)(2,1)S(1)}, u32[]{:S(2)}, u32[]{:S(2)}) %collective-permute-start.5) | collective-permute-done | bytes 131104 | tf_op jit(solution)/shard_map/ppermute | solution.py:627
  78.7 0.8 carry.1
  79.5 0.7 copy-done.1
  80.2 2.9 %collective-permute-start.6 = (bf16[1024,128]{1,0:T(8,128)(2,1)S(1)}, bf16[1024,128]{1,0:T(8,128)(2,1)S(1)}, u32[]{:S(2)}, u32[]{:S(2)}) collective-permute-start(bf16[1024,128]{1,0:T(8,128)(2,1)S(1)} %get-tuple-element.47), channel_id=1, source_target_pairs={{0,24},{8,16},{16,8},{24,0},{1,25},{9,17},{17,9},{25,1},{2,26},{10... | collective-permute-start | bytes 786440 | tf_op jit(solution)/shard_map/ppermute | solution.py:641
  83.0 1.0 %collective-permute-start.7 = (bf16[1024,128]{1,0:T(8,128)(2,1)S(1)}, bf16[1024,128]{1,0:T(8,128)(2,1)S(1)}, u32[]{:S(2)}, u32[]{:S(2)}) collective-permute-start(bf16[1024,128]{1,0:T(8,128)(2,1)S(1)} %get-tuple-element.48), channel_id=1, source_target_pairs={{0,16},{8,24},{16,0},{24,8},{1,17},{9,25},{17,1},{25,9},{2,18},{10... | collective-permute-start | bytes 786440 | tf_op jit(solution)/shard_map/ppermute | solution.py:641
  84.1 0.8 slice.15
  85.7 1.5 %correct.1 = bf16[4096,1024]{1,0:T(8,128)(2,1)} custom-call(s32[16]{0:T(128)} %get-tuple-element.27.meta, bf16[4096,1024]{1,0:T(8,128)(2,1)} %outputs.1.base_hbm, bf16[4096,128]{1,0:T(8,128)(2,1)} %get-tuple-element.31.c_ref, f32[16,4096]{1,0:T(8,128)} %get-tuple-element.35.carry_ref, bf16[128,1024]{1,0:T(8,128)(2,1)} %copy-done.1, ...), custom_call_target="tpu_custom_call", output_to_operand_aliasing={{}: (1, {})} | custom-call | flops 1073741824 | bytes 18874368 | tf_op jit(solution)/shard_map/correct/pallas_call | solution.py:643
  87.2 3.0 %collective-permute-done.6 = bf16[1024,128]{1,0:T(8,128)(2,1)S(1)} collective-permute-done((bf16[1024,128]{1,0:T(8,128)(2,1)S(1)}, bf16[1024,128]{1,0:T(8,128)(2,1)S(1)}, u32[]{:S(2)}, u32[]{:S(2)}) %collective-permute-start.6) | collective-permute-done | bytes 262176 | tf_op jit(solution)/shard_map/ppermute | solution.py:641
  90.2 5.1 %collective-permute-done.7 = bf16[1024,128]{1,0:T(8,128)(2,1)S(1)} collective-permute-done((bf16[1024,128]{1,0:T(8,128)(2,1)S(1)}, bf16[1024,128]{1,0:T(8,128)(2,1)S(1)}, u32[]{:S(2)}, u32[]{:S(2)}) %collective-permute-start.7) | collective-permute-done | bytes 262176 | tf_op jit(solution)/shard_map/ppermute | solution.py:641
  95.3 0.8 collective-permute-done.8
  96.4 4.2 %convert_add_fusion = f32[4,2,1024,128]{3,2,1,0:T(8,128)} fusion(bf16[4,2,1056,128]{3,2,1,0:T(8,128)(2,1)} %all-to-all-done, pred[2]{0:T(512)(128)(4,1)S(1)} %iota_compare_fusion, bf16[4,1024,128]{2,1,0:T(8,128)(2,1)S(1)} %select_select_fusion), kind=kLoop, calls=%fused_computation | loop fusion | flops 4194304 | bytes 7340034 | tf_op jit(solution)/shard_map/add | solution.py:667
  (22 shorter events, 2.1 us)
Async XLA Ops:
  1.4 3.2 %collective-permute-start = (bf16[16,1280]{1,0:T(8,128)(2,1)S(1)}, bf16[16,1280]{1,0:T(8,128)(2,1)S(1)}, u32[]{:S(2)}, u32[]{:S(2)}) collective-permute-start(bf16[16,1280]{1,0:T(8,128)(2,1)S(1)} %slice_bitcast_fusion), channel_id=1, source_target_pairs={{0,1},{1,2},{2,3},{3,4},{4,5},{5,6},{6,7},{8,9},{9,10},{10,11},{11... | collective-permute-start | bytes 122888 | tf_op jit(solution)/shard_map/ppermute | solution.py:30
  4.6 0.6 copy-start.4
  30.2 4.9 %collective-permute-start.1 = (bf16[144,1024]{1,0:T(8,128)(2,1)}, bf16[144,1024]{1,0:T(8,128)(2,1)S(1)}, u32[]{:S(2)}, u32[]{:S(2)}) collective-permute-start(bf16[144,1024]{1,0:T(8,128)(2,1)} %get-tuple-element.28.own_ref), channel_id=1, source_target_pairs={{0,1},{1,0},{2,3},{3,2},{4,5},{5,4},{6,7},{7,6},{8,9},{9,8},{10,11... | collective-permute-start | bytes 884744 | tf_op jit(solution)/shard_map/ppermute | solution.py:572
  35.1 1.0 copy-start
  43.2 35.5 %all-to-all-start = ((bf16[4,2,1056,128]{3,2,1,0:T(8,128)(2,1)}), bf16[4,2,1056,128]{3,2,1,0:T(8,128)(2,1)}, u32[]{:S(2)}, u32[]{:S(2)}) async-start(bf16[4,2,1056,128]{3,2,1,0:T(8,128)(2,1)} %bitcast.14), calls=%async_computation | async-start | bytes 4325376 | tf_op jit(solution)/shard_map/all_to_all | solution.py:614
  47.7 29.5 %collective-permute-start.2 = (bf16[144,512]{1,0:T(8,128)(2,1)S(1)}, bf16[144,512]{1,0:T(8,128)(2,1)S(1)}, u32[]{:S(2)}, u32[]{:S(2)}) collective-permute-start(bf16[144,512]{1,0:T(8,128)(2,1)S(1)} %pair.1), channel_id=1, source_target_pairs={{0,6},{1,7},{8,14},{9,15},{16,22},{17,23},{24,30},{25,31}} | collective-permute-start | bytes 442376 | tf_op jit(solution)/shard_map/ppermute | solution.py:30
  52.5 24.7 %collective-permute-start.3 = (bf16[144,512]{1,0:T(8,128)(2,1)S(1)}, bf16[144,512]{1,0:T(8,128)(2,1)S(1)}, u32[]{:S(2)}, u32[]{:S(2)}) collective-permute-start(bf16[144,512]{1,0:T(8,128)(2,1)S(1)} %pair.1), channel_id=1, source_target_pairs={{0,4},{1,5},{2,6},{3,7},{8,12},{9,13},{10,14},{11,15},{16,20},{17,... | collective-permute-start | bytes 442376 | tf_op jit(solution)/shard_map/ppermute | solution.py:30
  53.8 23.4 %collective-permute-start.4 = (bf16[144,512]{1,0:T(8,128)(2,1)S(1)}, bf16[144,512]{1,0:T(8,128)(2,1)S(1)}, u32[]{:S(2)}, u32[]{:S(2)}) collective-permute-start(bf16[144,512]{1,0:T(8,128)(2,1)S(1)} %pair.1), channel_id=1, source_target_pairs={{0,2},{1,3},{2,4},{3,5},{4,6},{5,7},{8,10},{9,11},{10,12},{11,13},... | collective-permute-start | bytes 442376 | tf_op jit(solution)/shard_map/ppermute | solution.py:30
  56.3 22.4 %copy-start.2 = (f32[8,1024]{1,0:T(8,128)S(1)}, f32[8,1024]{1,0:T(8,128)}, u32[]{:S(2)}) copy-start(f32[8,1024]{1,0:T(8,128)} %get-tuple-element.44.first_ref) | copy-start | bytes 98308
  56.3 22.4 %copy-start.3 = (s32[16]{0:T(128)S(1)}, s32[16]{0:T(128)}, u32[]{:S(2)}) copy-start(s32[16]{0:T(128)} %get-tuple-element.27.meta) | copy-start | bytes 196
  77.2 1.4 %collective-permute-start.5 = (bf16[128,512]{1,0:T(8,128)(2,1)S(1)}, bf16[128,512]{1,0:T(8,128)(2,1)S(1)}, u32[]{:S(2)}, u32[]{:S(2)}) collective-permute-start(bf16[128,512]{1,0:T(8,128)(2,1)S(1)} %prefix.1.mine_ref), channel_id=1, source_target_pairs={{0,1},{1,0},{2,3},{3,2},{4,5},{5,4},{6,7},{7,6},{8,9},{9,8},{10,11... | collective-permute-start | bytes 393224 | tf_op jit(solution)/shard_map/ppermute | solution.py:627
  79.5 0.7 copy-start.1
  80.2 10.1 %collective-permute-start.6 = (bf16[1024,128]{1,0:T(8,128)(2,1)S(1)}, bf16[1024,128]{1,0:T(8,128)(2,1)S(1)}, u32[]{:S(2)}, u32[]{:S(2)}) collective-permute-start(bf16[1024,128]{1,0:T(8,128)(2,1)S(1)} %get-tuple-element.47), channel_id=1, source_target_pairs={{0,24},{8,16},{16,8},{24,0},{1,25},{9,17},{17,9},{25,1},{2,26},{10... | collective-permute-start | bytes 786440 | tf_op jit(solution)/shard_map/ppermute | solution.py:641
  83.0 12.3 %collective-permute-start.7 = (bf16[1024,128]{1,0:T(8,128)(2,1)S(1)}, bf16[1024,128]{1,0:T(8,128)(2,1)S(1)}, u32[]{:S(2)}, u32[]{:S(2)}) collective-permute-start(bf16[1024,128]{1,0:T(8,128)(2,1)S(1)} %get-tuple-element.48), channel_id=1, source_target_pairs={{0,16},{8,24},{16,0},{24,8},{1,17},{9,25},{17,1},{25,9},{2,18},{10... | collective-permute-start | bytes 786440 | tf_op jit(solution)/shard_map/ppermute | solution.py:641
  84.1 12.1 %collective-permute-start.8 = (bf16[1024,128]{1,0:T(8,128)(2,1)S(1)}, bf16[1024,128]{1,0:T(8,128)(2,1)S(1)}, u32[]{:S(2)}, u32[]{:S(2)}) collective-permute-start(bf16[1024,128]{1,0:T(8,128)(2,1)S(1)} %get-tuple-element.49), channel_id=1, source_target_pairs={{0,8},{8,0},{16,24},{24,16},{1,9},{9,1},{17,25},{25,17},{2,10},{10... | collective-permute-start | bytes 786440 | tf_op jit(solution)/shard_map/ppermute | solution.py:641

commit v2 on v1

--- a/solution.py
+++ b/solution.py
@@ -307,7 +307,7 @@
             send(slot).wait()
 
 
-def output_kernel(origin, late, meta, act_ref, b_ref, c_ref, dt_ref, cum_ref, sin_ref, gain_in, rep_ref, rep16_ref, *refs):
+def output_kernel(origin, meta, act_ref, b_ref, c_ref, dt_ref, cum_ref, sin_ref, gain_in, rep_ref, rep16_ref, *refs):
     out_ref, gain_ref = refs[-2:]
     step = origin + pl.program_id(0)
     heads = dt_ref.shape[0]
@@ -337,9 +337,6 @@
         before = jnp.where(last_start(meta, begin) < begin, next_end(meta, begin), -1)
         entry = jnp.where(lane < before, jnp.exp2(cum), 0.0)
         entry = jnp.concatenate([entry, entry - entry.astype(BF16).astype(F32)], axis=0).T.astype(BF16)
-        if late:
-            extra = refs[0][:, rows]
-            extra = jnp.concatenate([extra, extra - extra.astype(BF16).astype(F32)], axis=0).T.astype(BF16)
         left_half = iota((CHUNK, 128), 1) < P_SIZE
         for quad in range(heads // 4):
             cols = slice(quad * 256, quad * 256 + 256)
@@ -360,10 +357,6 @@
                 sums.append(jnp.dot(mix, split, preferred_element_type=F32))
             inner = jnp.concatenate(sums, axis=1)
             value = inner + scale * outer + gain_ref[:, cols] * act_ref[rows, cols].astype(F32)
-            if late:
-                outer = jnp.dot(c_act, refs[1][:, cols], preferred_element_type=F32)
-                scale = jnp.dot(extra, rep16_ref[:, cols], preferred_element_type=F32)
-                value = value + scale * outer
             out_ref[rows, cols] = value.astype(BF16)
 
 
@@ -540,23 +533,23 @@
         step_size[0], log_decay[0], rep, rep16, tri,
     )
 
-    def outputs(first, last, late=()):
+    def outputs(first, last, *held):
         rows_of = functools.partial(pl.BlockSpec, index_map=lambda i, *_: (first + i, 0))
         heads_of = pl.BlockSpec((heads, BLOCK), lambda i, *_: (0, first + i))
         return pl.pallas_call(
-            functools.partial(output_kernel, first, bool(late)),
+            functools.partial(output_kernel, first),
             grid_spec=prefetch(
                 grid=(last - first,),
                 in_specs=[
                     rows_of((BLOCK, width)), rows_of((BLOCK, N)), rows_of((BLOCK, N)), heads_of, heads_of,
                     pl.BlockSpec((BLOCK // CHUNK, N, width), lambda i, *_: (first + i, 0, 0)),
                     smem, whole((heads, width)), whole((2 * heads, width)),
-                ] + ([heads_of, whole((N, width)), pl.BlockSpec(memory_space=pl.ANY)] if late else []),
+                ] + [in_hbm] * len(held),
                 out_specs=rows_of((BLOCK, width)),
                 scratch_shapes=[pltpu.VMEM((1, width), F32)],
             ),
             out_shape=jax.ShapeDtypeStruct((span, width), BF16),
-            input_output_aliases={13: 0} if late else {},
+            input_output_aliases={10: 0} if held else {},
             compiler_params=params(60),
             cost_estimate=pl.CostEstimate(
                 flops=2 * (last - first) * BLOCK * width * N * 4,
@@ -564,7 +557,7 @@
                 transcendentals=(last - first) * BLOCK * CHUNK * heads,
             ),
             name="outputs",
-        )(meta, act, b_act, c_act, step_size[0], cum, sin, skip_gain, rep, rep16, *late)
+        )(meta, act, b_act, c_act, step_size[0], cum, sin, skip_gain, rep, rep16, *held)
 
     side = width // 2
     count = lax.axis_size("seq")
@@ -578,8 +571,6 @@
         compiler_params=params(8),
         name="pair",
     )(shard, pay, early)
-    chips = count // 2
-    behind = [shifted(half, "seq", 2 * far) for far in range(chips - 1, 0, -1)]
     scanned, half = lax.optimization_barrier((sin, half))
     fin, first = pl.pallas_call(
         finals_kernel,
@@ -614,7 +605,11 @@
     got = lax.all_to_all(
         fin.reshape(owners, CAP, rows, N), "stream", split_axis=0, concat_axis=0, tiled=True
     )
-    base = outputs(0, steps)
+    base = outputs(0, 2)
+    half, base = lax.optimization_barrier((half, base))
+    chips = count // 2
+    behind = [shifted(half, "seq", 2 * far) for far in range(chips - 1, 0, -1)]
+    base = outputs(2, steps - 2, base)
     *behind, base = lax.optimization_barrier((*behind, base))
     mine = pl.pallas_call(
         prefix_kernel,
@@ -640,6 +635,8 @@
         swap = [(index, index ^ apart) for index in range(owners)]
         more.append(lax.ppermute(send[apart], "stream", swap))
 
+    carried, base = lax.optimization_barrier((carried, base))
+    base = outputs(steps - 2, steps, base)
     out = pl.pallas_call(
         correct_kernel,
         in_specs=[smem, in_hbm, whole((span, N)), whole((heads, span)), whole((N, width)), whole((2 * heads, width))],

time: 102 us -> 108 us (1.059)
  the two profiles are of different devices: /device:TPU:0 before, /device:TPU:1 now
where the time goes in v2:
time: 108 us; the launch traced here: 107 us
  Pallas kernels  69.2 us (64%)
  starting transfers between devices  24.1 us (22%)
  local copies, waits for them, and re-layouts  4.63 us (4%)
  other arithmetic  4.49 us (4%)
  waiting for transfers between devices  3.85 us (4%)
    pallas_call x3, Pallas kernels, outputs(): pl.pallas_call(functools.partial(output_kernel, first), grid_spec=prefetc...  27.5 us
    pallas_call x1, Pallas kernels, on_device(): pl.pallas_call(states_kernel, grid=(steps,), in_specs=[smem, smem, smem,...  24.5 us
    ppermute x4, starting transfers between devices, shifted(): lax.ppermute(value, axis, [(source, source + steps) for source in range(l...  15.6 us
    pallas_call x1, Pallas kernels, on_device(): pl.pallas_call(correct_kernel, in_specs=[smem, in_hbm, whole((span, N)),...  9.68 us
    pallas_call x1, Pallas kernels, on_device(): pl.pallas_call(finals_kernel, in_specs=[smem, in_hbm, in_hbm, in_hbm, in_...  6.31 us
    all_to_all x1, starting transfers between devices, on_device(): lax.all_to_all(fin.reshape(owners, CAP, rows, N), 'stream', split_axis=0,...  4.47 us
    add x1, other arithmetic, on_device(): ssm = got[:, :, :width].astype(F32) + extra.astype(F32)  4.18 us
    unnamed x11, local copies, waits for them, and re-layouts  2.96 us
  transfers between devices with their start and end apart: 10, of which 3 were waited for; matrix products, arithmetic and copies ran while one was open for 1% of the time, Pallas kernels for 35%

profile of v2, /device:TPU:1, one launch (start us, length us, event | category | flops | bytes accessed | tf_op | source)
XLA Modules:
  0.0 107.1 jit_solution(705840941520781245)
XLA Ops:
  0.6 0.8 slice_bitcast_fusion
  1.4 4.6 %collective-permute-start = (bf16[16,1280]{1,0:T(8,128)(2,1)S(1)}, bf16[16,1280]{1,0:T(8,128)(2,1)S(1)}, u32[]{:S(2)}, u32[]{:S(2)}) collective-permute-start(bf16[16,1280]{1,0:T(8,128)(2,1)S(1)} %slice_bitcast_fusion), channel_id=1, source_target_pairs={{0,1},{1,2},{2,3},{3,4},{4,5},{5,6},{6,7},{8,9},{9,10},{10,11},{11... | collective-permute-start | bytes 122888 | tf_op jit(solution)/shard_map/ppermute | solution.py:30
  6.0 1.1 %collective-permute-done.rim_ref = bf16[16,1280]{1,0:T(8,128)(2,1)S(1)} collective-permute-done((bf16[16,1280]{1,0:T(8,128)(2,1)S(1)}, bf16[16,1280]{1,0:T(8,128)(2,1)S(1)}, u32[]{:S(2)}, u32[]{:S(2)}) %collective-permute-start) | collective-permute-done | bytes 40992 | tf_op jit(solution)/shard_map/ppermute | solution.py:30
  7.7 24.5 %states.1 = (bf16[4096,1024]{1,0:T(8,128)(2,1)}, bf16[4096,128]{1,0:T(8,128)(2,1)}, bf16[4096,128]{1,0:T(8,128)(2,1)}, f32[16,4096]{1,0:T(8,128)}, f32[16,4096]{...) custom-call(s32[1]{0:T(128)} %bitcast.shard_ref, s32[1,32]{1,0:T(1,128)} %bounds.1, ...), custom_call_target="tpu_custom_call" | custom-call | flops 6291456000 | bytes 33554432 | tf_op jit(solution)/shard_map/states/pallas_call | solution.py:495
  32.3 1.8 %collective-permute-done.1.got_ref.early_ref = bf16[144,1024]{1,0:T(8,128)(2,1)S(1)} collective-permute-done((bf16[144,1024]{1,0:T(8,128)(2,1)}, bf16[144,1024]{1,0:T(8,128)(2,1)S(1)}, u32[]{:S(2)}, u32[]{:S(2)}) %collective-permute-start.1) | collective-permute-done | bytes 294944 | tf_op jit(solution)/shard_map/ppermute | solution.py:565
  34.0 1.0 copy-done
  35.1 6.3 %finals.1 = (bf16[8,1056,128]{2,1,0:T(8,128)(2,1)}, f32[8,1024]{1,0:T(8,128)}) custom-call(s32[16]{0:T(128)} %get-tuple-element.32.meta, bf16[4096,1024]{1,0:T(8,128)(2,1)} %get-tuple-element.33.act_hbm.act_ref, bf16[4096,128]{1,0:T(8,128)(2,1)} %get-tuple-element.34.b_hbm.b_ref, bf16[32,128,1024]{2,1,0:T(8,128)(2,1)} %get-tuple-element.42.sin_hbm.sin_ref, ...), custom_call_target="tpu_custom_call" | custom-call | flops 268435456 | bytes 6291456 | tf_op jit(solution)/shard_map/finals/pallas_call | solution.py:575
  41.4 4.5 %all-to-all-start = ((bf16[4,2,1056,128]{3,2,1,0:T(8,128)(2,1)}), bf16[4,2,1056,128]{3,2,1,0:T(8,128)(2,1)}, u32[]{:S(2)}, u32[]{:S(2)}) async-start(bf16[4,2,1056,128]{3,2,1,0:T(8,128)(2,1)} %bitcast.19), calls=%async_computation | async-start | bytes 4325376 | tf_op jit(solution)/shard_map/all_to_all | solution.py:605
  45.9 7.7 %outputs.3.refs_0_ = bf16[4096,1024]{1,0:T(8,128)(2,1)} custom-call(s32[16]{0:T(128)} %get-tuple-element.32.meta, bf16[4096,1024]{1,0:T(8,128)(2,1)} %get-tuple-element.33.act_hbm.act_ref, bf16[4096,128]{1,0:T(8,128)(2,1)} %get-tuple-element.34.b_hbm.b_ref, bf16[4096,128]{1,0:T(8,128)(2,1)} %get-tuple-element.35.c_ref, f32[16,4096]{1,0:T(8,128)} %bitcast.15, ...), custom_call_target="tpu_custom_call" | custom-call | flops 1073741824 | bytes 8388608 | tf_op jit(solution)/shard_map/outputs/pallas_call | solution.py:539
  53.6 7.5 %collective-permute-start.2 = (bf16[144,512]{1,0:T(8,128)(2,1)S(1)}, bf16[144,512]{1,0:T(8,128)(2,1)S(1)}, u32[]{:S(2)}, u32[]{:S(2)}) collective-permute-start(bf16[144,512]{1,0:T(8,128)(2,1)S(1)} %pair.1), channel_id=1, source_target_pairs={{0,6},{1,7},{8,14},{9,15},{16,22},{17,23},{24,30},{25,31}} | collective-permute-start | bytes 442376 | tf_op jit(solution)/shard_map/ppermute | solution.py:30
  61.1 1.3 %collective-permute-start.3 = (bf16[144,512]{1,0:T(8,128)(2,1)S(1)}, bf16[144,512]{1,0:T(8,128)(2,1)S(1)}, u32[]{:S(2)}, u32[]{:S(2)}) collective-permute-start(bf16[144,512]{1,0:T(8,128)(2,1)S(1)} %pair.1), channel_id=1, source_target_pairs={{0,4},{1,5},{2,6},{3,7},{8,12},{9,13},{10,14},{11,15},{16,20},{17,... | collective-permute-start | bytes 442376 | tf_op jit(solution)/shard_map/ppermute | solution.py:30
  62.4 2.2 %collective-permute-start.4 = (bf16[144,512]{1,0:T(8,128)(2,1)S(1)}, bf16[144,512]{1,0:T(8,128)(2,1)S(1)}, u32[]{:S(2)}, u32[]{:S(2)}) collective-permute-start(bf16[144,512]{1,0:T(8,128)(2,1)S(1)} %pair.1), channel_id=1, source_target_pairs={{0,2},{1,3},{2,4},{3,5},{4,6},{5,7},{8,10},{9,11},{10,12},{11,13},... | collective-permute-start | bytes 442376 | tf_op jit(solution)/shard_map/ppermute | solution.py:30
  64.6 12.1 %outputs.4.refs_0_ = bf16[4096,1024]{1,0:T(8,128)(2,1)} custom-call(s32[16]{0:T(128)} %get-tuple-element.32.meta, bf16[4096,1024]{1,0:T(8,128)(2,1)} %get-tuple-element.33.act_hbm.act_ref, bf16[4096,128]{1,0:T(8,128)(2,1)} %get-tuple-element.34.b_hbm.b_ref, bf16[4096,128]{1,0:T(8,128)(2,1)} %get-tuple-element.35.c_ref, ...), custom_call_target="tpu_custom_call", output_to_operand_aliasing={{}: (10, {})} | custom-call | flops 2147483648 | bytes 16777216 | tf_op jit(solution)/shard_map/outputs/pallas_call | solution.py:539
  76.9 1.1 %collective-permute-start.5 = (bf16[128,512]{1,0:T(8,128)(2,1)S(1)}, bf16[128,512]{1,0:T(8,128)(2,1)S(1)}, u32[]{:S(2)}, u32[]{:S(2)}) collective-permute-start(bf16[128,512]{1,0:T(8,128)(2,1)S(1)} %prefix.1.mine_ref), channel_id=1, source_target_pairs={{0,1},{1,0},{2,3},{3,2},{4,5},{5,4},{6,7},{7,6},{8,9},{9,8},{10,11... | collective-permute-start | bytes 393224 | tf_op jit(solution)/shard_map/ppermute | solution.py:622
  78.0 1.0 collective-permute-done.5.other_ref
  79.0 1.0 carry.1
  80.0 0.7 copy-done.1
  80.7 1.7 %collective-permute-start.8 = (bf16[1024,128]{1,0:T(8,128)(2,1)S(1)}, bf16[1024,128]{1,0:T(8,128)(2,1)S(1)}, u32[]{:S(2)}, u32[]{:S(2)}) collective-permute-start(bf16[1024,128]{1,0:T(8,128)(2,1)S(1)} %get-tuple-element.59), channel_id=1, source_target_pairs={{0,8},{8,0},{16,24},{24,16},{1,9},{9,1},{17,25},{25,17},{2,10},{10... | collective-permute-start | bytes 786440 | tf_op jit(solution)/shard_map/ppermute | solution.py:636
  82.4 1.2 %collective-permute-start.7 = (bf16[1024,128]{1,0:T(8,128)(2,1)S(1)}, bf16[1024,128]{1,0:T(8,128)(2,1)S(1)}, u32[]{:S(2)}, u32[]{:S(2)}) collective-permute-start(bf16[1024,128]{1,0:T(8,128)(2,1)S(1)} %get-tuple-element.58), channel_id=1, source_target_pairs={{0,16},{8,24},{16,0},{24,8},{1,17},{9,25},{17,1},{25,9},{2,18},{10... | collective-permute-start | bytes 786440 | tf_op jit(solution)/shard_map/ppermute | solution.py:636
  83.6 0.9 slice.15
  84.5 0.7 copy.19
  85.2 7.7 %outputs.5.base_hbm = bf16[4096,1024]{1,0:T(8,128)(2,1)} custom-call(s32[16]{0:T(128)} %get-tuple-element.32.meta, bf16[4096,1024]{1,0:T(8,128)(2,1)} %get-tuple-element.33.act_hbm.act_ref, bf16[4096,128]{1,0:T(8,128)(2,1)} %get-tuple-element.34.b_hbm.b_ref, bf16[4096,128]{1,0:T(8,128)(2,1)} %get-tuple-element.35.c_ref, ...), custom_call_target="tpu_custom_call", output_to_operand_aliasing={{}: (10, {})} | custom-call | flops 1073741824 | bytes 8388608 | tf_op jit(solution)/shard_map/outputs/pallas_call | solution.py:539
  92.9 9.7 %correct.1 = bf16[4096,1024]{1,0:T(8,128)(2,1)} custom-call(s32[16]{0:T(128)} %get-tuple-element.32.meta, bf16[4096,1024]{1,0:T(8,128)(2,1)} %outputs.5.base_hbm, bf16[4096,128]{1,0:T(8,128)(2,1)} %get-tuple-element.35.c_ref, f32[16,4096]{1,0:T(8,128)} %get-tuple-element.40.carry_ref, bf16[128,1024]{1,0:T(8,128)(2,1)} %copy-done.1, ...), custom_call_target="tpu_custom_call", output_to_operand_aliasing={{}: (1, {})} | custom-call | flops 1073741824 | bytes 18874368 | tf_op jit(solution)/shard_map/correct/pallas_call | solution.py:640
  102.9 4.2 %convert_add_fusion = f32[4,2,1024,128]{3,2,1,0:T(8,128)} fusion(bf16[4,2,1056,128]{3,2,1,0:T(8,128)(2,1)} %all-to-all-done, pred[2]{0:T(512)(128)(4,1)S(1)} %iota_compare_fusion, bf16[4,1024,128]{2,1,0:T(8,128)(2,1)S(1)} %select_select_fusion), kind=kLoop, calls=%fused_computation | loop fusion | flops 4194304 | bytes 7340034 | tf_op jit(solution)/shard_map/add | solution.py:664
  (24 shorter events, 1.2 us)
Async XLA Ops:
  1.4 5.7 %collective-permute-start = (bf16[16,1280]{1,0:T(8,128)(2,1)S(1)}, bf16[16,1280]{1,0:T(8,128)(2,1)S(1)}, u32[]{:S(2)}, u32[]{:S(2)}) collective-permute-start(bf16[16,1280]{1,0:T(8,128)(2,1)S(1)} %slice_bitcast_fusion), channel_id=1, source_target_pairs={{0,1},{1,2},{2,3},{3,4},{4,5},{5,6},{6,7},{8,9},{9,10},{10,11},{11... | collective-permute-start | bytes 122888 | tf_op jit(solution)/shard_map/ppermute | solution.py:30
  7.1 0.6 copy-start.4
  32.2 1.9 %collective-permute-start.1 = (bf16[144,1024]{1,0:T(8,128)(2,1)}, bf16[144,1024]{1,0:T(8,128)(2,1)S(1)}, u32[]{:S(2)}, u32[]{:S(2)}) collective-permute-start(bf16[144,1024]{1,0:T(8,128)(2,1)} %get-tuple-element.38.own_ref), channel_id=1, source_target_pairs={{0,1},{1,0},{2,3},{3,2},{4,5},{5,4},{6,7},{7,6},{8,9},{9,8},{10,11... | collective-permute-start | bytes 884744 | tf_op jit(solution)/shard_map/ppermute | solution.py:565
  34.0 1.0 copy-start
  41.4 37.6 %all-to-all-start = ((bf16[4,2,1056,128]{3,2,1,0:T(8,128)(2,1)}), bf16[4,2,1056,128]{3,2,1,0:T(8,128)(2,1)}, u32[]{:S(2)}, u32[]{:S(2)}) async-start(bf16[4,2,1056,128]{3,2,1,0:T(8,128)(2,1)} %bitcast.19), calls=%async_computation | async-start | bytes 4325376 | tf_op jit(solution)/shard_map/all_to_all | solution.py:605
  53.6 25.4 %copy-start.2 = (f32[8,1024]{1,0:T(8,128)S(1)}, f32[8,1024]{1,0:T(8,128)}, u32[]{:S(2)}) copy-start(f32[8,1024]{1,0:T(8,128)} %get-tuple-element.51.first_ref) | copy-start | bytes 98308
  53.6 25.4 %copy-start.3 = (s32[16]{0:T(128)S(1)}, s32[16]{0:T(128)}, u32[]{:S(2)}) copy-start(s32[16]{0:T(128)} %get-tuple-element.32.meta) | copy-start | bytes 196
  53.6 23.2 %collective-permute-start.2 = (bf16[144,512]{1,0:T(8,128)(2,1)S(1)}, bf16[144,512]{1,0:T(8,128)(2,1)S(1)}, u32[]{:S(2)}, u32[]{:S(2)}) collective-permute-start(bf16[144,512]{1,0:T(8,128)(2,1)S(1)} %pair.1), channel_id=1, source_target_pairs={{0,6},{1,7},{8,14},{9,15},{16,22},{17,23},{24,30},{25,31}} | collective-permute-start | bytes 442376 | tf_op jit(solution)/shard_map/ppermute | solution.py:30
  61.1 15.6 %collective-permute-start.3 = (bf16[144,512]{1,0:T(8,128)(2,1)S(1)}, bf16[144,512]{1,0:T(8,128)(2,1)S(1)}, u32[]{:S(2)}, u32[]{:S(2)}) collective-permute-start(bf16[144,512]{1,0:T(8,128)(2,1)S(1)} %pair.1), channel_id=1, source_target_pairs={{0,4},{1,5},{2,6},{3,7},{8,12},{9,13},{10,14},{11,15},{16,20},{17,... | collective-permute-start | bytes 442376 | tf_op jit(solution)/shard_map/ppermute | solution.py:30
  62.4 14.3 %collective-permute-start.4 = (bf16[144,512]{1,0:T(8,128)(2,1)S(1)}, bf16[144,512]{1,0:T(8,128)(2,1)S(1)}, u32[]{:S(2)}, u32[]{:S(2)}) collective-permute-start(bf16[144,512]{1,0:T(8,128)(2,1)S(1)} %pair.1), channel_id=1, source_target_pairs={{0,2},{1,3},{2,4},{3,5},{4,6},{5,7},{8,10},{9,11},{10,12},{11,13},... | collective-permute-start | bytes 442376 | tf_op jit(solution)/shard_map/ppermute | solution.py:30
  76.9 2.1 %collective-permute-start.5 = (bf16[128,512]{1,0:T(8,128)(2,1)S(1)}, bf16[128,512]{1,0:T(8,128)(2,1)S(1)}, u32[]{:S(2)}, u32[]{:S(2)}) collective-permute-start(bf16[128,512]{1,0:T(8,128)(2,1)S(1)} %prefix.1.mine_ref), channel_id=1, source_target_pairs={{0,1},{1,0},{2,3},{3,2},{4,5},{5,4},{6,7},{7,6},{8,9},{9,8},{10,11... | collective-permute-start | bytes 393224 | tf_op jit(solution)/shard_map/ppermute | solution.py:622
  80.0 0.7 copy-start.1
  80.7 21.9 %collective-permute-start.8 = (bf16[1024,128]{1,0:T(8,128)(2,1)S(1)}, bf16[1024,128]{1,0:T(8,128)(2,1)S(1)}, u32[]{:S(2)}, u32[]{:S(2)}) collective-permute-start(bf16[1024,128]{1,0:T(8,128)(2,1)S(1)} %get-tuple-element.59), channel_id=1, source_target_pairs={{0,8},{8,0},{16,24},{24,16},{1,9},{9,1},{17,25},{25,17},{2,10},{10... | collective-permute-start | bytes 786440 | tf_op jit(solution)/shard_map/ppermute | solution.py:636
  82.4 20.2 %collective-permute-start.7 = (bf16[1024,128]{1,0:T(8,128)(2,1)S(1)}, bf16[1024,128]{1,0:T(8,128)(2,1)S(1)}, u32[]{:S(2)}, u32[]{:S(2)}) collective-permute-start(bf16[1024,128]{1,0:T(8,128)(2,1)S(1)} %get-tuple-element.58), channel_id=1, source_target_pairs={{0,16},{8,24},{16,0},{24,8},{1,17},{9,25},{17,1},{25,9},{2,18},{10... | collective-permute-start | bytes 786440 | tf_op jit(solution)/shard_map/ppermute | solution.py:636
  83.6 19.0 %collective-permute-start.6 = (bf16[1024,128]{1,0:T(8,128)(2,1)S(1)}, bf16[1024,128]{1,0:T(8,128)(2,1)S(1)}, u32[]{:S(2)}, u32[]{:S(2)}) collective-permute-start(bf16[1024,128]{1,0:T(8,128)(2,1)S(1)} %get-tuple-element.57), channel_id=1, source_target_pairs={{0,24},{8,16},{16,8},{24,0},{1,25},{9,17},{17,9},{25,1},{2,26},{10... | collective-permute-start | bytes 786440 | tf_op jit(solution)/shard_map/ppermute | solution.py:636

commit v3 on v2

--- a/solution.py
+++ b/solution.py
@@ -222,7 +222,7 @@
     width = rep_ref.shape[1]
 
     def place(slot):
-        return pl.multiple_of((jnp.minimum(meta[1 + slot], span) - 1) // CHUNK * CHUNK, CHUNK)
+        return pl.multiple_of((meta[1 + slot] - 1) // CHUNK * CHUNK, CHUNK)
 
     def copies(slot):
         low = place(slot)
@@ -237,9 +237,15 @@
             for index, (source, target) in enumerate(pairs)
         ]
 
-    fetched = [copies(slot) for slot in range(EMAX)]
-    for copy in sum(fetched, []):
-        copy.start()
+    def fetch(slot, _):
+        for copy in copies(slot):
+            copy.start()
+        return 0
+
+    found = jnp.int32(0)
+    for slot in range(EMAX):
+        found = found + (meta[1 + slot] <= span).astype(jnp.int32)
+    lax.fori_loop(0, found, fetch, 0)
     blank[...] = jnp.zeros_like(blank)
     blanks = [
         pltpu.make_async_copy(blank, fin_hbm.at[index], blank_sem.at[index])
@@ -247,12 +253,16 @@
     ]
     for copy in blanks:
         copy.start()
+    first_ref[...] = jnp.zeros_like(first_ref)
     lines[...] = jnp.zeros_like(lines)
-    for copy in sum(fetched, []):
+    for copy in blanks:
         copy.wait()
-    for slot in range(EMAX):
+
+    def finish(slot, _):
+        for copy in copies(slot):
+            copy.wait()
         end = meta[1 + slot]
-        start = meta[slot]
+        start = jnp.where(slot > 0, meta[jnp.maximum(slot, 1)], meta[0])
         low = place(slot)
         there = pl.ds(low, CHUNK)
         lane = iota((heads, CHUNK), 1) + low
@@ -266,9 +276,13 @@
         local = outer_dot(b_held[slot], load)
         through = spread_row(jnp.where(start < low, jnp.exp2(at_end), 0.0), rep_ref[...])
         final = local + through * sin_held[slot].astype(F32)
-        if slot == 0:
+        target = meta[5 + slot]
+
+        @pl.when((slot == 0) & (start < 0))
+        def _():
             opened = jnp.sum(jnp.where(lane == end - 1, carry_ref[:, there], 0.0), axis=1, keepdims=True)
             first_ref[...] = jnp.broadcast_to(spread_row(opened, rep_ref[...]), first_ref.shape)
+
         row = iota((16, CHUNK), 0)
         col = iota((16, CHUNK), 1) + low
         pick = (col == end - 3 + row) & (col >= start) & (row < 3)
@@ -283,28 +297,26 @@
         for index in range(3):
             for tile in range(tiles):
                 at = index * tiles + tile
-                lines[slot, at : at + 1] = last[index : index + 1, tile * 128 : tile * 128 + 128]
-
-        made[slot, :width] = final.astype(BF16).T
-        made[slot, width:] = lines[slot].astype(BF16)
-    for copy in blanks:
-        copy.wait()
-    used = [(meta[1 + slot] <= span) & (meta[5 + slot] >= 0) for slot in range(EMAX)]
-
-    def send(slot):
-        return pltpu.make_async_copy(made.at[slot], fin_hbm.at[meta[5 + slot]], made_sem.at[slot])
-
-    for slot in range(EMAX):
-
-        @pl.when(used[slot])
+                lines[at : at + 1] = last[index : index + 1, tile * 128 : tile * 128 + 128]
+
+        @pl.when(target >= 0)
         def _():
-            send(slot).start()
-
-    for slot in range(EMAX):
-
-        @pl.when(used[slot])
+            made[slot, :width] = final.astype(BF16).T
+            made[slot, width:] = lines[...].astype(BF16)
+            pltpu.make_async_copy(made.at[slot], fin_hbm.at[target], made_sem.at[slot]).start()
+
+        return 0
+
+    lax.fori_loop(0, found, finish, 0)
+
+    def close(slot, _):
+        @pl.when(meta[5 + slot] >= 0)
         def _():
-            send(slot).wait()
+            pltpu.make_async_copy(made.at[slot], fin_hbm.at[meta[5 + slot]], made_sem.at[slot]).wait()
+
+        return 0
+
+    lax.fori_loop(0, found, close, 0)
 
 
 def output_kernel(origin, meta, act_ref, b_ref, c_ref, dt_ref, cum_ref, sin_ref, gain_in, rep_ref, rep16_ref, *refs):
@@ -571,6 +583,8 @@
         compiler_params=params(8),
         name="pair",
     )(shard, pay, early)
+    chips = count // 2
+    behind = [shifted(half, "seq", 2 * far) for far in range(chips - 1, 0, -1)]
     scanned, half = lax.optimization_barrier((sin, half))
     fin, first = pl.pallas_call(
         finals_kernel,
@@ -592,7 +606,7 @@
             pltpu.VMEM((EMAX, 16, channels), BF16),
             pltpu.VMEM((rows, N), BF16),
             pltpu.VMEM((EMAX, rows, N), BF16),
-            pltpu.VMEM((EMAX, TAIL, N), F32),
+            pltpu.VMEM((TAIL, N), F32),
             pltpu.SemaphoreType.DMA((EMAX, 5)),
             pltpu.SemaphoreType.DMA((slots,)),
             pltpu.SemaphoreType.DMA((EMAX,)),
@@ -605,11 +619,7 @@
     got = lax.all_to_all(
         fin.reshape(owners, CAP, rows, N), "stream", split_axis=0, concat_axis=0, tiled=True
     )
-    base = outputs(0, 2)
-    half, base = lax.optimization_barrier((half, base))
-    chips = count // 2
-    behind = [shifted(half, "seq", 2 * far) for far in range(chips - 1, 0, -1)]
-    base = outputs(2, steps - 2, base)
+    base = outputs(0, steps - 2)
     *behind, base = lax.optimization_barrier((*behind, base))
     mine = pl.pallas_call(
         prefix_kernel,

time: 108 us -> 103 us (0.954)
  the two profiles are of different devices: /device:TPU:1 before, /device:TPU:5 now
where the time goes in v3:
time: 103 us; the launch traced here: 102 us
  Pallas kernels  62.7 us (61%)
  starting transfers between devices  25 us (24%)
  local copies, waits for them, and re-layouts  4.63 us (4%)
  other arithmetic  4.49 us (4%)
  waiting for transfers between devices  4.18 us (4%)
    pallas_call x1, Pallas kernels, on_device(): pl.pallas_call(states_kernel, grid=(steps,), in_specs=[smem, smem, smem,...  24.5 us
    pallas_call x2, Pallas kernels, outputs(): pl.pallas_call(functools.partial(output_kernel, first), grid_spec=prefetc...  24.2 us
    ppermute x4, starting transfers between devices, shifted(): lax.ppermute(value, axis, [(source, source + steps) for source in range(l...  12.3 us
    all_to_all x1, starting transfers between devices, on_device(): lax.all_to_all(fin.reshape(owners, CAP, rows, N), 'stream', split_axis=0,...  9.97 us
    pallas_call x1, Pallas kernels, on_device(): pl.pallas_call(correct_kernel, in_specs=[smem, in_hbm, whole((span, N)),...  9.68 us
    add x1, other arithmetic, on_device(): ssm = got[:, :, :width].astype(F32) + extra.astype(F32)  4.18 us
    pallas_call x1, Pallas kernels, on_device(): pl.pallas_call(finals_kernel, in_specs=[smem, in_hbm, in_hbm, in_hbm, in_...  3.4 us
    unnamed x11, local copies, waits for them, and re-layouts  2.96 us
  transfers between devices with their start and end apart: 10, of which 3 were waited for; matrix products, arithmetic and copies ran while one was open for 2% of the time, Pallas kernels for 33%

profile of v3, /device:TPU:5, one launch (start us, length us, event | category | flops | bytes accessed | tf_op | source)
XLA Modules:
  0.0 101.9 jit_solution(2923998174609788114)
XLA Ops:
  0.6 0.8 slice_bitcast_fusion
  1.4 3.8 %collective-permute-start = (bf16[16,1280]{1,0:T(8,128)(2,1)S(1)}, bf16[16,1280]{1,0:T(8,128)(2,1)S(1)}, u32[]{:S(2)}, u32[]{:S(2)}) collective-permute-start(bf16[16,1280]{1,0:T(8,128)(2,1)S(1)} %slice_bitcast_fusion), channel_id=1, source_target_pairs={{0,1},{1,2},{2,3},{3,4},{4,5},{5,6},{6,7},{8,9},{9,10},{10,11},{11... | collective-permute-start | bytes 122888 | tf_op jit(solution)/shard_map/ppermute | solution.py:30
  5.2 1.1 %collective-permute-done.rim_ref = bf16[16,1280]{1,0:T(8,128)(2,1)S(1)} collective-permute-done((bf16[16,1280]{1,0:T(8,128)(2,1)S(1)}, bf16[16,1280]{1,0:T(8,128)(2,1)S(1)}, u32[]{:S(2)}, u32[]{:S(2)}) %collective-permute-start) | collective-permute-done | bytes 40992 | tf_op jit(solution)/shard_map/ppermute | solution.py:30
  6.3 0.6 copy-done.4
  6.9 24.5 %states.1 = (bf16[4096,1024]{1,0:T(8,128)(2,1)}, bf16[4096,128]{1,0:T(8,128)(2,1)}, bf16[4096,128]{1,0:T(8,128)(2,1)}, f32[16,4096]{1,0:T(8,128)}, f32[16,4096]{...) custom-call(s32[1]{0:T(128)} %bitcast.shard_ref, s32[1,32]{1,0:T(1,128)} %bounds.1, ...), custom_call_target="tpu_custom_call" | custom-call | flops 6291456000 | bytes 33554432 | tf_op jit(solution)/shard_map/states/pallas_call | solution.py:507
  31.4 1.8 %collective-permute-done.1.got_ref.early_ref = bf16[144,1024]{1,0:T(8,128)(2,1)S(1)} collective-permute-done((bf16[144,1024]{1,0:T(8,128)(2,1)}, bf16[144,1024]{1,0:T(8,128)(2,1)S(1)}, u32[]{:S(2)}, u32[]{:S(2)}) %collective-permute-start.1) | collective-permute-done | bytes 294944 | tf_op jit(solution)/shard_map/ppermute | solution.py:577
  33.2 1.0 copy-done
  34.2 3.4 %finals.1 = (bf16[8,1056,128]{2,1,0:T(8,128)(2,1)}, f32[8,1024]{1,0:T(8,128)}) custom-call(s32[16]{0:T(128)} %get-tuple-element.29.meta, bf16[4096,1024]{1,0:T(8,128)(2,1)} %get-tuple-element.30.act_hbm.act_ref, bf16[4096,128]{1,0:T(8,128)(2,1)} %get-tuple-element.31.b_hbm.b_ref, bf16[32,128,1024]{2,1,0:T(8,128)(2,1)} %get-tuple-element.39.sin_hbm.sin_ref, ...), custom_call_target="tpu_custom_call" | custom-call | flops 268435456 | bytes 6291456 | tf_op jit(solution)/shard_map/finals/pallas_call | solution.py:589
  37.6 10.0 %all-to-all-start = ((bf16[4,2,1056,128]{3,2,1,0:T(8,128)(2,1)}), bf16[4,2,1056,128]{3,2,1,0:T(8,128)(2,1)}, u32[]{:S(2)}, u32[]{:S(2)}) async-start(bf16[4,2,1056,128]{3,2,1,0:T(8,128)(2,1)} %bitcast.18), calls=%async_computation | async-start | bytes 4325376 | tf_op jit(solution)/shard_map/all_to_all | solution.py:619
  47.6 5.0 %collective-permute-start.2 = (bf16[144,512]{1,0:T(8,128)(2,1)S(1)}, bf16[144,512]{1,0:T(8,128)(2,1)S(1)}, u32[]{:S(2)}, u32[]{:S(2)}) collective-permute-start(bf16[144,512]{1,0:T(8,128)(2,1)S(1)} %pair.1), channel_id=1, source_target_pairs={{0,6},{1,7},{8,14},{9,15},{16,22},{17,23},{24,30},{25,31}} | collective-permute-start | bytes 442376 | tf_op jit(solution)/shard_map/ppermute | solution.py:30
  52.7 1.3 %collective-permute-start.3 = (bf16[144,512]{1,0:T(8,128)(2,1)S(1)}, bf16[144,512]{1,0:T(8,128)(2,1)S(1)}, u32[]{:S(2)}, u32[]{:S(2)}) collective-permute-start(bf16[144,512]{1,0:T(8,128)(2,1)S(1)} %pair.1), channel_id=1, source_target_pairs={{0,4},{1,5},{2,6},{3,7},{8,12},{9,13},{10,14},{11,15},{16,20},{17,... | collective-permute-start | bytes 442376 | tf_op jit(solution)/shard_map/ppermute | solution.py:30
  54.0 2.2 %collective-permute-start.4 = (bf16[144,512]{1,0:T(8,128)(2,1)S(1)}, bf16[144,512]{1,0:T(8,128)(2,1)S(1)}, u32[]{:S(2)}, u32[]{:S(2)}) collective-permute-start(bf16[144,512]{1,0:T(8,128)(2,1)S(1)} %pair.1), channel_id=1, source_target_pairs={{0,2},{1,3},{2,4},{3,5},{4,6},{5,7},{8,10},{9,11},{10,12},{11,13},... | collective-permute-start | bytes 442376 | tf_op jit(solution)/shard_map/ppermute | solution.py:30
  56.2 16.5 %outputs.2.refs_0_ = bf16[4096,1024]{1,0:T(8,128)(2,1)} custom-call(s32[16]{0:T(128)} %get-tuple-element.29.meta, bf16[4096,1024]{1,0:T(8,128)(2,1)} %get-tuple-element.30.act_hbm.act_ref, bf16[4096,128]{1,0:T(8,128)(2,1)} %get-tuple-element.31.b_hbm.b_ref, bf16[4096,128]{1,0:T(8,128)(2,1)} %get-tuple-element.32.c_ref, f32[16,4096]{1,0:T(8,128)} %bitcast.16, ...), custom_call_target="tpu_custom_call" | custom-call | flops 3221225472 | bytes 25165824 | tf_op jit(solution)/shard_map/outputs/pallas_call | solution.py:551
  72.9 1.3 %collective-permute-done.5.other_ref = bf16[128,512]{1,0:T(8,128)(2,1)S(1)} collective-permute-done((bf16[128,512]{1,0:T(8,128)(2,1)S(1)}, bf16[128,512]{1,0:T(8,128)(2,1)S(1)}, u32[]{:S(2)}, u32[]{:S(2)}) %collective-permute-start.5) | collective-permute-done | bytes 131104 | tf_op jit(solution)/shard_map/ppermute | solution.py:632
  74.2 0.9 carry.1
  75.1 0.7 copy-done.1
  75.8 1.1 %collective-permute-start.8 = (bf16[1024,128]{1,0:T(8,128)(2,1)S(1)}, bf16[1024,128]{1,0:T(8,128)(2,1)S(1)}, u32[]{:S(2)}, u32[]{:S(2)}) collective-permute-start(bf16[1024,128]{1,0:T(8,128)(2,1)S(1)} %get-tuple-element.53), channel_id=1, source_target_pairs={{0,8},{8,0},{16,24},{24,16},{1,9},{9,1},{17,25},{25,17},{2,10},{10... | collective-permute-start | bytes 786440 | tf_op jit(solution)/shard_map/ppermute | solution.py:646
  76.9 0.6 collective-permute-start.7
  77.5 0.9 collective-permute-start.6
  78.4 0.8 slice.15
  79.3 0.7 copy.18
  80.0 7.7 %outputs.3.base_hbm = bf16[4096,1024]{1,0:T(8,128)(2,1)} custom-call(s32[16]{0:T(128)} %get-tuple-element.29.meta, bf16[4096,1024]{1,0:T(8,128)(2,1)} %get-tuple-element.30.act_hbm.act_ref, bf16[4096,128]{1,0:T(8,128)(2,1)} %get-tuple-element.31.b_hbm.b_ref, bf16[4096,128]{1,0:T(8,128)(2,1)} %get-tuple-element.32.c_ref, ...), custom_call_target="tpu_custom_call", output_to_operand_aliasing={{}: (10, {})} | custom-call | flops 1073741824 | bytes 8388608 | tf_op jit(solution)/shard_map/outputs/pallas_call | solution.py:551
  87.7 9.7 %correct.1 = bf16[4096,1024]{1,0:T(8,128)(2,1)} custom-call(s32[16]{0:T(128)} %get-tuple-element.29.meta, bf16[4096,1024]{1,0:T(8,128)(2,1)} %outputs.3.base_hbm, bf16[4096,128]{1,0:T(8,128)(2,1)} %get-tuple-element.32.c_ref, f32[16,4096]{1,0:T(8,128)} %get-tuple-element.37.carry_ref, bf16[128,1024]{1,0:T(8,128)(2,1)} %copy-done.1, ...), custom_call_target="tpu_custom_call", output_to_operand_aliasing={{}: (1, {})} | custom-call | flops 1073741824 | bytes 18874368 | tf_op jit(solution)/shard_map/correct/pallas_call | solution.py:650
  97.7 4.2 %convert_add_fusion = f32[4,2,1024,128]{3,2,1,0:T(8,128)} fusion(bf16[4,2,1056,128]{3,2,1,0:T(8,128)(2,1)} %all-to-all-done, pred[2]{0:T(512)(128)(4,1)S(1)} %iota_compare_fusion, bf16[4,1024,128]{2,1,0:T(8,128)(2,1)S(1)} %select_select_fusion), kind=kLoop, calls=%fused_computation | loop fusion | flops 4194304 | bytes 7340034 | tf_op jit(solution)/shard_map/add | solution.py:674
  (23 shorter events, 0.7 us)
Async XLA Ops:
  1.4 4.8 %collective-permute-start = (bf16[16,1280]{1,0:T(8,128)(2,1)S(1)}, bf16[16,1280]{1,0:T(8,128)(2,1)S(1)}, u32[]{:S(2)}, u32[]{:S(2)}) collective-permute-start(bf16[16,1280]{1,0:T(8,128)(2,1)S(1)} %slice_bitcast_fusion), channel_id=1, source_target_pairs={{0,1},{1,2},{2,3},{3,4},{4,5},{5,6},{6,7},{8,9},{9,10},{10,11},{11... | collective-permute-start | bytes 122888 | tf_op jit(solution)/shard_map/ppermute | solution.py:30
  6.3 0.6 copy-start.4
  31.3 1.9 %collective-permute-start.1 = (bf16[144,1024]{1,0:T(8,128)(2,1)}, bf16[144,1024]{1,0:T(8,128)(2,1)S(1)}, u32[]{:S(2)}, u32[]{:S(2)}) collective-permute-start(bf16[144,1024]{1,0:T(8,128)(2,1)} %get-tuple-element.35.own_ref), channel_id=1, source_target_pairs={{0,1},{1,0},{2,3},{3,2},{4,5},{5,4},{6,7},{7,6},{8,9},{9,8},{10,11... | collective-permute-start | bytes 884744 | tf_op jit(solution)/shard_map/ppermute | solution.py:577
  33.2 1.0 copy-start
  37.6 36.6 %all-to-all-start = ((bf16[4,2,1056,128]{3,2,1,0:T(8,128)(2,1)}), bf16[4,2,1056,128]{3,2,1,0:T(8,128)(2,1)}, u32[]{:S(2)}, u32[]{:S(2)}) async-start(bf16[4,2,1056,128]{3,2,1,0:T(8,128)(2,1)} %bitcast.18), calls=%async_computation | async-start | bytes 4325376 | tf_op jit(solution)/shard_map/all_to_all | solution.py:619
  47.6 25.1 %collective-permute-start.2 = (bf16[144,512]{1,0:T(8,128)(2,1)S(1)}, bf16[144,512]{1,0:T(8,128)(2,1)S(1)}, u32[]{:S(2)}, u32[]{:S(2)}) collective-permute-start(bf16[144,512]{1,0:T(8,128)(2,1)S(1)} %pair.1), channel_id=1, source_target_pairs={{0,6},{1,7},{8,14},{9,15},{16,22},{17,23},{24,30},{25,31}} | collective-permute-start | bytes 442376 | tf_op jit(solution)/shard_map/ppermute | solution.py:30
  52.7 20.0 %collective-permute-start.3 = (bf16[144,512]{1,0:T(8,128)(2,1)S(1)}, bf16[144,512]{1,0:T(8,128)(2,1)S(1)}, u32[]{:S(2)}, u32[]{:S(2)}) collective-permute-start(bf16[144,512]{1,0:T(8,128)(2,1)S(1)} %pair.1), channel_id=1, source_target_pairs={{0,4},{1,5},{2,6},{3,7},{8,12},{9,13},{10,14},{11,15},{16,20},{17,... | collective-permute-start | bytes 442376 | tf_op jit(solution)/shard_map/ppermute | solution.py:30
  54.0 18.7 %collective-permute-start.4 = (bf16[144,512]{1,0:T(8,128)(2,1)S(1)}, bf16[144,512]{1,0:T(8,128)(2,1)S(1)}, u32[]{:S(2)}, u32[]{:S(2)}) collective-permute-start(bf16[144,512]{1,0:T(8,128)(2,1)S(1)} %pair.1), channel_id=1, source_target_pairs={{0,2},{1,3},{2,4},{3,5},{4,6},{5,7},{8,10},{9,11},{10,12},{11,13},... | collective-permute-start | bytes 442376 | tf_op jit(solution)/shard_map/ppermute | solution.py:30
  56.2 18.0 %copy-start.2 = (f32[8,1024]{1,0:T(8,128)S(1)}, f32[8,1024]{1,0:T(8,128)}, u32[]{:S(2)}) copy-start(f32[8,1024]{1,0:T(8,128)} %get-tuple-element.45.first_ref) | copy-start | bytes 98308
  56.2 18.0 %copy-start.3 = (s32[16]{0:T(128)S(1)}, s32[16]{0:T(128)}, u32[]{:S(2)}) copy-start(s32[16]{0:T(128)} %get-tuple-element.29.meta) | copy-start | bytes 196
  72.8 1.4 %collective-permute-start.5 = (bf16[128,512]{1,0:T(8,128)(2,1)S(1)}, bf16[128,512]{1,0:T(8,128)(2,1)S(1)}, u32[]{:S(2)}, u32[]{:S(2)}) collective-permute-start(bf16[128,512]{1,0:T(8,128)(2,1)S(1)} %prefix.1.mine_ref), channel_id=1, source_target_pairs={{0,1},{1,0},{2,3},{3,2},{4,5},{5,4},{6,7},{7,6},{8,9},{9,8},{10,11... | collective-permute-start | bytes 393224 | tf_op jit(solution)/shard_map/ppermute | solution.py:632
  75.1 0.7 copy-start.1
  75.8 21.6 %collective-permute-start.8 = (bf16[1024,128]{1,0:T(8,128)(2,1)S(1)}, bf16[1024,128]{1,0:T(8,128)(2,1)S(1)}, u32[]{:S(2)}, u32[]{:S(2)}) collective-permute-start(bf16[1024,128]{1,0:T(8,128)(2,1)S(1)} %get-tuple-element.53), channel_id=1, source_target_pairs={{0,8},{8,0},{16,24},{24,16},{1,9},{9,1},{17,25},{25,17},{2,10},{10... | collective-permute-start | bytes 786440 | tf_op jit(solution)/shard_map/ppermute | solution.py:646
  76.9 20.5 %collective-permute-start.7 = (bf16[1024,128]{1,0:T(8,128)(2,1)S(1)}, bf16[1024,128]{1,0:T(8,128)(2,1)S(1)}, u32[]{:S(2)}, u32[]{:S(2)}) collective-permute-start(bf16[1024,128]{1,0:T(8,128)(2,1)S(1)} %get-tuple-element.52), channel_id=1, source_target_pairs={{0,16},{8,24},{16,0},{24,8},{1,17},{9,25},{17,1},{25,9},{2,18},{10... | collective-permute-start | bytes 786440 | tf_op jit(solution)/shard_map/ppermute | solution.py:646
  77.5 19.9 %collective-permute-start.6 = (bf16[1024,128]{1,0:T(8,128)(2,1)S(1)}, bf16[1024,128]{1,0:T(8,128)(2,1)S(1)}, u32[]{:S(2)}, u32[]{:S(2)}) collective-permute-start(bf16[1024,128]{1,0:T(8,128)(2,1)S(1)} %get-tuple-element.51), channel_id=1, source_target_pairs={{0,24},{8,16},{16,8},{24,0},{1,25},{9,17},{17,9},{25,1},{2,26},{10... | collective-permute-start | bytes 786440 | tf_op jit(solution)/shard_map/ppermute | solution.py:646
